TPU v7x, 256 devices: a whole 4x4x8 slice. The times are simulated.
256 devices in a mesh: lon: 32 (over x_lo, z, core), head: 4 (over y), cfg: 2 (over x_hi).
Axes of the slice: x: 4 (x_hi: 2, x_lo: 2; x = x_hi * 2 + x_lo), y: 4, z: 8, core: 2. Of those that a mesh axis runs over, the one named last changes fastest.
Arguments:
- latents: bfloat16 [2, 2, 48, 192, 1536], P('cfg', None, None, 'lon', 'head'), may hold values from -14 to 14
- timestep: int32 [1], replicated, may hold values from 0 to 999
- guide_num: int32 [1], replicated, may hold values from 20 to 80
- guide_den: int32 [1], replicated, may hold values from 10 to 20
- depth_level: int32 [2, 48, 192], P(None, None, 'lon'), may hold values from 0 to 15
- depth_table: bfloat16 [16, 1536], replicated, may hold values from -6 to 6
- time_weight: bfloat16 [256, 3072], replicated, may hold values from -0.375 to 0.375
- base_q: bfloat16 [1536, 1536], P(None, 'head'), may hold values from -1 to 1
- base_k: bfloat16 [1536, 1536], P(None, 'head'), may hold values from -1 to 1
- base_v: bfloat16 [1536, 1536], P(None, 'head'), may hold values from -0.15625 to 0.15625
- base_o: bfloat16 [1536, 1536], P('head'), may hold values from -0.15625 to 0.15625
- ctrl_q: bfloat16 [1536, 1536], P(None, 'head'), may hold values from -1 to 1
- ctrl_k: bfloat16 [1536, 1536], P(None, 'head'), may hold values from -1 to 1
- ctrl_v: bfloat16 [1536, 1536], P(None, 'head'), may hold values from -0.15625 to 0.15625
- ctrl_o: bfloat16 [1536, 1536], P('head'), may hold values from -0.15625 to 0.15625
- zero_linear: bfloat16 [1536, 1536], P('head'), may hold values from -0.15625 to 0.15625
Outputs:
- guided: bfloat16 [2, 48, 192, 1536], P(None, None, 'lon', ('head', 'cfg'))
All inputs are finite; a program needn't handle non-finite values.
Results may differ from a plain program's by a relative error of at most 0.022.
Values may be sent and summed in bfloat16 or wider, within the bound.
A program may use at most 128 MiB of HBM per device.

v0:
```python
import functools
import math

import jax
import jax.numpy as jnp
from jax import lax
from jax.experimental import pallas as pl
from jax.experimental.pallas import tpu as pltpu
from jax.sharding import PartitionSpec as P

HD = 64
FREQ = 256
PAIR = 2 * HD
GROUP = 2
BASE, CTRL = 0, 1
F32 = jnp.float32
BF16 = jnp.bfloat16
MESH = pl.DeviceIdType.MESH


def embed_time(timestep):
    half_count = FREQ // 2
    freqs = jnp.exp(-math.log(10000.0) * jnp.arange(half_count).astype(F32) / half_count)
    angles = timestep.astype(F32)[0] * freqs
    temb = jnp.concatenate([jnp.cos(angles), jnp.sin(angles)]).astype(BF16)
    return jnp.broadcast_to(temb[None, :], (16, FREQ))


def attend_pair(q, k, v):
    rows = q.shape[0]
    low = lax.broadcasted_iota(jnp.int32, (rows, PAIR), 1) < HD
    zero = jnp.zeros_like(q)
    both = jnp.concatenate([jnp.where(low, q, zero), jnp.where(low, zero, q)], axis=0)
    scores = lax.dot_general(both, k, (((1,), (1,)), ((), ())), preferred_element_type=F32)
    top = jnp.max(scores, axis=1, keepdims=True)
    expo = jnp.exp2(scores - top).astype(BF16)
    ones = jnp.concatenate([v, jnp.ones_like(v)], axis=1)
    mixed = jnp.dot(expo, ones, preferred_element_type=F32)
    mixed = mixed[:, :PAIR] / mixed[:, PAIR:]
    return jnp.where(low, mixed[:rows], mixed[rows:]).astype(BF16)


def kernel(
    dims,
    x_hbm,
    temb_ref,
    ratio_ref,
    onehot_ref,
    table_ref,
    tw_hbm,
    bq_hbm,
    bk_hbm,
    bv_hbm,
    bo_hbm,
    cq_hbm,
    ck_hbm,
    cv_hbm,
    co_hbm,
    zl_hbm,
    out_ref,
    xg,
    tw,
    wqkv,
    wo,
    mod,
    ms,
    q,
    kv,
    att,
    csum,
    part,
    r1,
    r2,
    kept,
    give,
    take,
    load_sem,
    g_send,
    g_recv,
    h_send,
    h_recv,
    s1_send,
    s1_recv,
    s2_send,
    s2_recv,
    c_send,
    c_recv,
):
    frames, rows, cols, feat, n_lon, n_head = dims
    C = frames * rows
    T = C * cols
    width = feat * n_head
    groups = cols // GROUP
    G = GROUP * C
    lon, head, cfg = lax.axis_index("lon"), lax.axis_index("head"), lax.axis_index("cfg")
    is_cond = cfg == 0
    hp, hm, ho = lax.rem(head + 1, n_head), lax.rem(head + n_head - 1, n_head), lax.rem(head + 2, n_head)
    lp, lm = lax.rem(lon + 1, n_lon), lax.rem(lon + n_lon - 1, n_lon)
    to_hp, to_hm = (lon, hp, cfg), (lon, hm, cfg)
    to_lp, to_lm = (lp, head, cfg), (lm, head, cfg)
    to_cfg = (lon, head, 1 - cfg)

    own_copy = pltpu.make_async_copy(x_hbm, xg.at[head], load_sem.at[0])
    own_copy.start()
    loads = [
        (tw_hbm, tw),
        (cq_hbm, wqkv.at[CTRL, :, pl.ds(0, feat)]),
        (ck_hbm, wqkv.at[CTRL, :, pl.ds(feat, feat)]),
        (cv_hbm, wqkv.at[CTRL, :, pl.ds(2 * feat, feat)]),
        (bq_hbm, wqkv.at[BASE, :, pl.ds(0, feat)]),
        (bk_hbm, wqkv.at[BASE, :, pl.ds(feat, feat)]),
        (bv_hbm, wqkv.at[BASE, :, pl.ds(2 * feat, feat)]),
        (co_hbm, wo.at[CTRL]),
        (bo_hbm, wo.at[BASE]),
        (zl_hbm, wo.at[2]),
    ]
    loads = [pltpu.make_async_copy(s, d, load_sem.at[i + 1]) for i, (s, d) in enumerate(loads)]

    barrier = pltpu.get_barrier_semaphore()
    for who in (to_hp, to_hm, to_lp, to_lm, to_cfg):
        pl.semaphore_signal(barrier, inc=1, device_id=who, device_id_type=MESH)
    for copy in loads:
        copy.start()
    pl.semaphore_wait(barrier, 5)
    own_copy.wait()

    def send(src, dst, ssem, rsem, who):
        return pltpu.make_async_remote_copy(
            src_ref=src, dst_ref=dst, send_sem=ssem, recv_sem=rsem, device_id=who, device_id_type=MESH
        )

    def gather(slot, c, kind, who):
        place = xg.at[slot, :, c]
        return send(place, place, g_send.at[kind, c], g_recv.at[kind, c], who)

    def own_sends(c):
        gather(head, c, 0, to_hp).start()
        gather(head, c, 1, to_hm).start()

    def serve(c):
        gather(hm, c, 0, to_hp).wait_recv()
        gather(hp, c, 1, to_hm).wait_recv()
        if c % 2 == 0:
            gather(hm, c, 2, to_hp).start()
        else:
            gather(hp, c, 2, to_hm).start()
        if c + 3 < cols:
            own_sends(c + 3)

    def halo(branch, g, side, row0):
        src = kv.at[branch, pl.ds(T + row0, G)]
        dst = kv.at[branch, pl.ds((0 if side == 0 else 2 * T) + row0, G)]
        who = to_lp if side == 0 else to_lm
        return send(src, dst, h_send.at[branch, g, side], h_recv.at[branch, g, side], who)

    def normalise(branch, c, at):
        parts = [xg[j, :, c].reshape(C, feat).astype(F32) for j in range(n_head)]
        if branch == CTRL:
            hot = onehot_ref[pl.ds(c * C, C), :]
            for j in range(n_head):
                emb = jnp.dot(hot, table_ref[:, j * feat : (j + 1) * feat], preferred_element_type=F32)
                parts[j] = parts[j] + emb
        center = sum(jnp.sum(u, axis=1, keepdims=True) for u in parts) * (1.0 / width)
        parts = [u - center for u in parts]
        spread = sum(jnp.sum(u * u, axis=1, keepdims=True) for u in parts) * (1.0 / width)
        scale = lax.rsqrt(spread + 1e-06)
        for j in range(n_head):
            sl = pl.ds(j * feat, feat)
            gain = 1.0 + mod[0:1, sl]
            shift = mod[0:1, pl.ds(width + j * feat, feat)]
            ms[branch, pl.ds(at, C), sl] = (parts[j] * scale * gain + shift).astype(BF16)

    def project(branch, g):
        for c in range(GROUP):
            normalise(branch, g * GROUP + c, c * C)
        row0 = g * G
        normed = ms[branch]
        query = jnp.dot(normed, wqkv[branch, :, :feat], preferred_element_type=F32)
        q[branch, pl.ds(row0, G), :] = (query * (math.log2(math.e) / math.sqrt(HD))).astype(BF16)
        kv[branch, pl.ds(T + row0, G), :] = jnp.dot(
            normed, wqkv[branch, :, feat:], preferred_element_type=F32
        ).astype(BF16)

    for c in range(3):
        own_sends(c)
    loads[0].wait()
    mod[...] = jnp.dot(temb_ref[...], tw[...], preferred_element_type=F32)
    for copy in loads[1:]:
        copy.wait()

    served = 0
    for g in range(groups):
        until = min(cols, (g + 2) * GROUP)
        for c in range(served, until):
            serve(c)
        served = until
        for c in range(g * GROUP, (g + 1) * GROUP):
            gather(ho, c, 2, to_hp).wait_recv()

        @pl.when(is_cond)
        def _():
            project(CTRL, g)
            for side in range(2):
                halo(CTRL, g, side, g * G).start()

        project(BASE, g)

        @pl.when(jnp.logical_not(is_cond))
        def _():
            for side in range(2):
                halo(BASE, g, side, g * G).start()

    @pl.when(is_cond)
    def _():
        for g in range(groups):
            for side in range(2):
                halo(BASE, g, side, g * G).start()

    half = C // 2

    def stage1(j, way):
        src = part.at[j, ho, pl.ds(way * half, half)]
        return send(src, r1.at[j, way], s1_send.at[j, way], s1_recv.at[j, way], to_hp if way == 0 else to_hm)

    def stage2(j, way):
        src = part.at[j, hp if way == 0 else hm]
        return send(src, r2.at[j, way], s2_send.at[j, way], s2_recv.at[j, way], to_hp if way == 0 else to_hm)

    def swap(c):
        return send(give.at[c], take.at[c], c_send.at[c], c_recv.at[c], to_cfg)

    def finish(c, mine, other):
        ratio = ratio_ref[0]
        cond = jnp.where(is_cond, mine, other)
        uncond = jnp.where(is_cond, other, mine)
        res = (uncond + ratio * (cond - uncond)).astype(BF16)
        out_ref[:, c] = res.reshape(frames, rows, feat // 2)

    first = jnp.where(is_cond, 0, cols)

    def wait_halo(branch, g, side):
        halo(branch, g, side, g * G).wait_recv()

    @pl.loop(first, 2 * cols + 2)
    def _(i):
        @pl.when(i < 2 * cols)
        def _():
            branch = jnp.where(i < cols, CTRL, BASE)
            c = jnp.where(i < cols, i, i - cols)

            @pl.when(c == 0)
            def _():
                for g in range(groups):
                    wait_halo(branch, g, 0)

            @pl.when(lax.rem(c, GROUP) == 0)
            def _():
                wait_halo(branch, lax.div(c, GROUP), 1)

            r0 = pl.multiple_of(c * C, C)
            n_keys = (2 * cols + 1) * C
            for p in range(feat // PAIR):
                sl = pl.ds(p * PAIR, PAIR)
                att[:, sl] = attend_pair(
                    q[branch, pl.ds(r0, C), sl],
                    kv[branch, pl.ds(r0, n_keys), sl],
                    kv[branch, pl.ds(r0, n_keys), pl.ds(feat + p * PAIR, PAIR)],
                )

            with_ctrl = jnp.logical_and(is_cond, i >= cols)

            @pl.when(with_ctrl)
            def _():
                for d in range(n_head):
                    sl = pl.ds(d * feat, feat)
                    both = jnp.dot(att[...], wo[BASE, :, sl], preferred_element_type=F32)
                    both += jnp.dot(csum[c], wo[2, :, sl], preferred_element_type=F32)
                    part[i, d] = both.astype(BF16)

            @pl.when(jnp.logical_not(with_ctrl))
            def _():
                for d in range(n_head):
                    sl = pl.ds(d * feat, feat)
                    part[i, d] = jnp.dot(att[...], wo[branch, :, sl], preferred_element_type=F32).astype(BF16)

            stage1(i, 0).start()
            stage1(i, 1).start()

        j = i - 1

        @pl.when(jnp.logical_and(j >= first, j < 2 * cols))
        def _():
            stage1(j, 0).wait_recv()
            part[j, hp, pl.ds(0, half)] = (part[j, hp, pl.ds(0, half)].astype(F32) + r1[j, 0].astype(F32)).astype(BF16)
            stage2(j, 0).start()
            stage1(j, 1).wait_recv()
            part[j, hm, pl.ds(half, half)] = (
                part[j, hm, pl.ds(half, half)].astype(F32) + r1[j, 1].astype(F32)
            ).astype(BF16)
            stage2(j, 1).start()

        n = i - 2

        @pl.when(n >= first)
        def _():
            stage2(n, 0).wait_recv()
            stage2(n, 1).wait_recv()
            total = part[n, head].astype(F32) + r2[n, 0].astype(F32) + r2[n, 1].astype(F32)

            @pl.when(n < cols)
            def _():
                csum[n] = total.astype(BF16)

            @pl.when(n >= cols)
            def _():
                c = n - cols
                block = xg[head, :, c].reshape(C, feat).astype(F32) + total
                low, high = block[:, : feat // 2], block[:, feat // 2 :]
                give[c] = jnp.where(is_cond, high, low).astype(BF16)
                swap(c).start()
                mine = jnp.where(is_cond, low, high)

                @pl.when(is_cond)
                def _():
                    swap(c).wait_recv()
                    finish(c, mine, take[c].astype(F32))

                @pl.when(jnp.logical_not(is_cond))
                def _():
                    kept[c] = mine

    @pl.when(jnp.logical_not(is_cond))
    def _():
        @pl.loop(0, cols)
        def _(c):
            swap(c).wait_recv()
            finish(c, kept[c], take[c].astype(F32))

    for c in range(cols):
        gather(head, c, 0, to_hp).wait_send()
        gather(head, c, 1, to_hm).wait_send()
        gather(hm, c, 2, to_hp).wait_send()

    for g in range(groups):
        for side in range(2):
            halo(BASE, g, side, g * G).wait_send()

    @pl.when(is_cond)
    def _():
        for g in range(groups):
            for side in range(2):
                halo(CTRL, g, side, g * G).wait_send()

    @pl.loop(first, 2 * cols)
    def _(j):
        for way in range(2):
            stage1(j, way).wait_send()
            stage2(j, way).wait_send()

    @pl.loop(0, cols)
    def _(c):
        swap(c).wait_send()


def local(
    latents,
    timestep,
    guide_num,
    guide_den,
    depth_level,
    depth_table,
    time_weight,
    base_q,
    base_k,
    base_v,
    base_o,
    ctrl_q,
    ctrl_k,
    ctrl_v,
    ctrl_o,
    zero_linear,
):
    x = latents[0].transpose(0, 2, 1, 3)
    frames, cols, rows, feat = x.shape
    n_lon, n_head = lax.axis_size("lon"), lax.axis_size("head")
    C, T, width = frames * rows, frames * rows * cols, feat * n_head
    levels = depth_table.shape[0]
    temb = embed_time(timestep)
    ratio = guide_num.astype(F32) / guide_den.astype(F32)
    onehot = (depth_level.transpose(2, 0, 1).reshape(T, 1) == jnp.arange(levels)).astype(BF16)
    dma = pltpu.SemaphoreType.DMA
    vmem = pl.BlockSpec(memory_space=pltpu.VMEM)
    smem = pl.BlockSpec(memory_space=pltpu.SMEM)
    hbm = pl.BlockSpec(memory_space=pl.ANY)
    groups = cols // GROUP
    out = pl.pallas_call(
        functools.partial(kernel, (frames, rows, cols, feat, n_lon, n_head)),
        out_shape=jax.ShapeDtypeStruct((frames, cols, rows, feat // 2), BF16),
        in_specs=[hbm, vmem, smem, vmem, vmem] + [hbm] * 10,
        out_specs=vmem,
        scratch_shapes=[
            pltpu.VMEM((n_head, frames, cols, rows, feat), BF16),
            pltpu.VMEM((FREQ, 2 * width), BF16),
            pltpu.VMEM((2, width, 3 * feat), BF16),
            pltpu.VMEM((3, feat, width), BF16),
            pltpu.VMEM((16, 2 * width), F32),
            pltpu.VMEM((2, GROUP * C, width), BF16),
            pltpu.VMEM((2, T, feat), BF16),
            pltpu.VMEM((2, 3 * T, 2 * feat), BF16),
            pltpu.VMEM((C, feat), BF16),
            pltpu.VMEM((cols, C, feat), BF16),
            pltpu.VMEM((2 * cols, n_head, C, feat), BF16),
            pltpu.VMEM((2 * cols, 2, C // 2, feat), BF16),
            pltpu.VMEM((2 * cols, 2, C, feat), BF16),
            pltpu.VMEM((cols, C, feat // 2), F32),
            pltpu.VMEM((cols, C, feat // 2), BF16),
            pltpu.VMEM((cols, C, feat // 2), BF16),
            dma((11,)),
            dma((3, cols)),
            dma((3, cols)),
            dma((2, groups, 2)),
            dma((2, groups, 2)),
            dma((2 * cols, 2)),
            dma((2 * cols, 2)),
            dma((2 * cols, 2)),
            dma((2 * cols, 2)),
            dma((cols,)),
            dma((cols,)),
        ],
        compiler_params=pltpu.CompilerParams(
            collective_id=0, has_side_effects=True, vmem_limit_bytes=58 * 1024 * 1024
        ),
    )(
        x,
        temb,
        ratio,
        onehot,
        depth_table,
        time_weight,
        base_q,
        base_k,
        base_v,
        base_o,
        ctrl_q,
        ctrl_k,
        ctrl_v,
        ctrl_o,
        zero_linear,
    )
    return out.transpose(0, 2, 1, 3)


def solution(mesh):
    return jax.shard_map(
        local,
        mesh=mesh,
        in_specs=(
            P("cfg", None, None, "lon", "head"),
            P(),
            P(),
            P(),
            P(None, None, "lon"),
            P(),
            P(),
            P(None, "head"),
            P(None, "head"),
            P(None, "head"),
            P("head", None),
            P(None, "head"),
            P(None, "head"),
            P(None, "head"),
            P("head", None),
            P("head", None),
        ),
        out_specs=P(None, None, "lon", ("head", "cfg")),
        check_vma=False,
    )
```

profile of v0, /device:TPU:4, one launch (start us, length us, event | category | flops | bytes accessed | tf_op | source)
XLA Modules:
  0.0 91.0 jit_solution(11700435292900665168)
XLA Ops:
  2.1 0.8 eq.15
  2.8 0.6 broadcast_in_dim.2.temb_ref
  3.4 0.8 fusion.onehot_ref
  4.2 85.0 %shard_map.154 = bf16[2,6,48,192]{3,2,1,0:T(8,128)(2,1)} custom-call(bf16[2,6,48,384]{3,2,1,0:T(8,128)(2,1)} %bitcast.7, bf16[16,256]{1,0:T(8,128)(2,1)} %broadcast_in_dim.2.temb_ref, f32[1]{0:T(128)S(6)} %div.11.ratio_ref, bf16[576,16]{1,0:T(8,128)(2,1)} %fusion.onehot_ref, bf16[16,1536]{1,0:T(8,128)(2,1)} %table_ref.1, bf16[256,3072]{1,0:T(8,128)(2,1)} %tw_hbm.1, ...), custom_call_target="tpu_custom_call" | custom-call | tf_op jit(solution)/shard_map/pallas_call | solution.py:396
  89.3 1.7 %copy.21 = bf16[2,48,6,192]{3,1,2,0:T(8,128)(2,1)} copy(bf16[2,48,6,192]{3,1,2,0:T(8,128)(2,1)} %bitcast.6) | data formatting | bytes 442368
  (2 shorter events, 0.1 us)
where the time goes:
time: 92.6 us; the launch traced here: 91 us
  Pallas kernels  85 us (92%)
  local copies, waits for them, and re-layouts  3.06 us (3%)
  between operations  2 us (2%)
    pallas_call x1, Pallas kernels, local(): pl.pallas_call(functools.partial(kernel, (frames, rows, cols, feat, n_lon...  85 us

commit v1 on v0

v1 whole, which is shorter than its diff:
```python
import functools
import math

import jax
import jax.numpy as jnp
from jax import lax
from jax.experimental import pallas as pl
from jax.experimental.pallas import tpu as pltpu
from jax.sharding import PartitionSpec as P

HD = 64
FREQ = 256
PAIR = 2 * HD
GROUP = 2
BASE, CTRL = 0, 1
F32 = jnp.float32
BF16 = jnp.bfloat16
MESH = pl.DeviceIdType.MESH


def attend_pair(q, k, v):
    rows = q.shape[0]
    low = lax.broadcasted_iota(jnp.int32, (rows, PAIR), 1) < HD
    zero = jnp.zeros_like(q)
    both = jnp.concatenate([jnp.where(low, q, zero), jnp.where(low, zero, q)], axis=0)
    scores = lax.dot_general(both, k, (((1,), (1,)), ((), ())), preferred_element_type=F32)
    top = jnp.max(scores, axis=1, keepdims=True)
    expo = jnp.exp2(scores - top).astype(BF16)
    ones = jnp.concatenate([v, jnp.ones_like(v)], axis=1)
    mixed = jnp.dot(expo, ones, preferred_element_type=F32)
    mixed = mixed[:, :PAIR] / mixed[:, PAIR:]
    return jnp.where(low, mixed[:rows], mixed[rows:]).astype(BF16)


def kernel(
    dims,
    x_hbm,
    step_ref,
    num_ref,
    den_ref,
    level_ref,
    freq_ref,
    table_ref,
    tw_hbm,
    bq_hbm,
    bk_hbm,
    bv_hbm,
    bo_hbm,
    cq_hbm,
    ck_hbm,
    cv_hbm,
    co_hbm,
    zl_hbm,
    out_ref,
    xg,
    tw,
    wqkv,
    wo,
    mod,
    ms,
    q,
    kv,
    att,
    csum,
    part,
    r1,
    r2,
    kept,
    give,
    take,
    load_sem,
    g_send,
    g_recv,
    h_send,
    h_recv,
    s1_send,
    s1_recv,
    s2_send,
    s2_recv,
    f_send,
    f_recv,
):
    frames, rows, cols, feat, n_lon, n_head = dims
    C = frames * rows
    T = C * cols
    width = feat * n_head
    groups = cols // GROUP
    G = GROUP * C
    lon, head, cfg = lax.axis_index("lon"), lax.axis_index("head"), lax.axis_index("cfg")
    is_cond = cfg == 0
    hp, hm, ho = lax.rem(head + 1, n_head), lax.rem(head + n_head - 1, n_head), lax.rem(head + 2, n_head)
    lp, lm = lax.rem(lon + 1, n_lon), lax.rem(lon + n_lon - 1, n_lon)
    to_hp, to_hm = (lon, hp, cfg), (lon, hm, cfg)
    to_lp, to_lm = (lp, head, cfg), (lm, head, cfg)
    half_feat = feat // 2
    heads = [head, hp, ho, hm]

    own_copy = pltpu.make_async_copy(x_hbm, xg.at[head], load_sem.at[0])
    own_copy.start()
    loads = [
        (tw_hbm, tw),
        (cq_hbm, wqkv.at[CTRL, :, pl.ds(0, feat)]),
        (ck_hbm, wqkv.at[CTRL, :, pl.ds(feat, feat)]),
        (cv_hbm, wqkv.at[CTRL, :, pl.ds(2 * feat, feat)]),
        (bq_hbm, wqkv.at[BASE, :, pl.ds(0, feat)]),
        (bk_hbm, wqkv.at[BASE, :, pl.ds(feat, feat)]),
        (bv_hbm, wqkv.at[BASE, :, pl.ds(2 * feat, feat)]),
    ]
    for at, w in ((CTRL, co_hbm), (BASE, bo_hbm), (2, zl_hbm)):
        loads += [(w.at[:, pl.ds(d * feat, feat)], wo.at[at, d]) for d in range(n_head)]
    loads = [pltpu.make_async_copy(s, d, load_sem.at[i + 1]) for i, (s, d) in enumerate(loads)]

    barrier = pltpu.get_barrier_semaphore()
    group = [(lon, h, cfg) for h in heads[1:]] + [(lon, h, 1 - cfg) for h in heads]
    for who in group + [to_lp, to_lm]:
        pl.semaphore_signal(barrier, inc=1, device_id=who, device_id_type=MESH)
    for copy in loads:
        copy.start()
    pl.semaphore_wait(barrier, len(group) + 2)

    def send(src, dst, ssem, rsem, who):
        return pltpu.make_async_remote_copy(
            src_ref=src, dst_ref=dst, send_sem=ssem, recv_sem=rsem, device_id=who, device_id_type=MESH
        )

    def gather(slot, c, kind, who):
        place = xg.at[slot, :, c]
        return send(place, place, g_send.at[kind, c], g_recv.at[kind, c], who)

    def own_send(c, kind, who):
        return send(x_hbm.at[:, c], xg.at[head, :, c], g_send.at[kind, c], g_recv.at[kind, c], who)

    def own_sends(c):
        own_send(c, 0, to_hp).start()
        own_send(c, 1, to_hm).start()

    def serve(c):
        gather(hm, c, 0, to_hp).wait_recv()
        gather(hp, c, 1, to_hm).wait_recv()
        if c % 2 == 0:
            gather(hm, c, 2, to_hp).start()
        else:
            gather(hp, c, 2, to_hm).start()
        if c + 3 < cols:
            own_sends(c + 3)

    def halo(branch, g, side, row0):
        src = kv.at[branch, pl.ds(T + row0, G)]
        dst = kv.at[branch, pl.ds((0 if side == 0 else 2 * T) + row0, G)]
        who = to_lp if side == 0 else to_lm
        return send(src, dst, h_send.at[branch, g, side], h_recv.at[branch, g, side], who)

    def normalise(branch, c, at):
        parts = [xg[j, :, c].reshape(C, feat).astype(F32) for j in range(n_head)]
        if branch == CTRL:
            levels = lax.broadcasted_iota(jnp.int32, (table_ref.shape[0], rows), 0)
            hot = [jnp.where(levels == level_ref[c, f : f + 1, :], 1.0, 0.0).astype(BF16) for f in range(frames)]
            for j in range(n_head):
                table = table_ref[:, j * feat : (j + 1) * feat]
                emb = [
                    lax.dot_general(h, table, (((0,), (0,)), ((), ())), preferred_element_type=F32) for h in hot
                ]
                parts[j] = parts[j] + jnp.concatenate(emb, axis=0)
        center = sum(jnp.sum(u, axis=1, keepdims=True) for u in parts) * (1.0 / width)
        parts = [u - center for u in parts]
        spread = sum(jnp.sum(u * u, axis=1, keepdims=True) for u in parts) * (1.0 / width)
        scale = lax.rsqrt(spread + 1e-06)
        for j in range(n_head):
            sl = pl.ds(j * feat, feat)
            gain = 1.0 + mod[0:1, sl]
            shift = mod[0:1, pl.ds(width + j * feat, feat)]
            ms[branch, pl.ds(at, C), sl] = (parts[j] * scale * gain + shift).astype(BF16)

    def project(branch, g):
        for c in range(GROUP):
            normalise(branch, g * GROUP + c, c * C)
        row0 = g * G
        normed = ms[branch]
        query = jnp.dot(normed, wqkv[branch, :, :feat], preferred_element_type=F32)
        q[branch, pl.ds(row0, G), :] = (query * (math.log2(math.e) / math.sqrt(HD))).astype(BF16)
        kv[branch, pl.ds(T + row0, G), :] = jnp.dot(
            normed, wqkv[branch, :, feat:], preferred_element_type=F32
        ).astype(BF16)

    for c in range(3):
        own_sends(c)

    @pl.when(jnp.logical_not(is_cond))
    def _():
        csum[...] = jnp.zeros_like(csum)

    angles = freq_ref[...] * step_ref[0].astype(F32)
    temb = jnp.concatenate([jnp.cos(angles), jnp.sin(angles)], axis=1).astype(BF16)
    loads[0].wait()
    mod[...] = jnp.dot(temb, tw[...], preferred_element_type=F32)
    ones = jnp.ones((8, feat), F32)
    ratio = (ones * num_ref[0].astype(F32)) / (ones * den_ref[0].astype(F32))
    factor = jnp.where(is_cond, ratio, 1.0 - ratio)[0:1, :]
    own_copy.wait()
    for copy in loads[1:]:
        copy.wait()

    served = 0
    for g in range(groups):
        until = min(cols, (g + 2) * GROUP)
        for c in range(served, until):
            serve(c)
        served = until
        for c in range(g * GROUP, (g + 1) * GROUP):
            gather(ho, c, 2, to_hp).wait_recv()

        @pl.when(is_cond)
        def _():
            project(CTRL, g)
            for side in range(2):
                halo(CTRL, g, side, g * G).start()

        project(BASE, g)

        @pl.when(jnp.logical_not(is_cond))
        def _():
            for side in range(2):
                halo(BASE, g, side, g * G).start()

    @pl.when(is_cond)
    def _():
        for g in range(groups):
            for side in range(2):
                halo(BASE, g, side, g * G).start()

    def stage1(j, way):
        src = part.at[j, ho, pl.ds(way * C, C)]
        return send(src, r1.at[j, way], s1_send.at[j, way], s1_recv.at[j, way], to_hp if way == 0 else to_hm)

    def stage2(j, way):
        src = part.at[j, hp if way == 0 else hm]
        return send(src, r2.at[j, way], s2_send.at[j, way], s2_recv.at[j, way], to_hp if way == 0 else to_hm)

    def relay(j):
        for way, d in ((0, hp), (1, hm)):
            stage1(j, way).wait_recv()
            sl = pl.ds(way * C, C)
            part[j, d, sl] = (part[j, d, sl].astype(F32) + r1[j, way].astype(F32)).astype(BF16)
            stage2(j, way).start()

    def collect(j):
        stage2(j, 0).wait_recv()
        stage2(j, 1).wait_recv()
        total = part[j, head].astype(F32) + r2[j, 0].astype(F32) + r2[j, 1].astype(F32)
        csum[j] = total.astype(BF16)

    def final(c, k, side):
        there = (n_head - k) % n_head
        return send(
            give.at[c, k, side],
            take.at[c, there, cfg],
            f_send.at[c, k, side],
            f_recv.at[c, there, cfg],
            (lon, heads[k], side),
        )

    def final_in(c, k, side):
        return send(
            give.at[c, k, side], take.at[c, k, side], f_send.at[c, k, side], f_recv.at[c, k, side], to_hp
        )

    def finish(c):
        total = kept[c]
        for k in range(1, n_head):
            for side in range(2):
                final_in(c, k, side).wait_recv()
                total = total + take[c, k, side].astype(F32)
        final_in(c, 0, 1 - cfg).wait_recv()
        total = total + take[c, 0, 1 - cfg].astype(F32)
        out_ref[:, c] = total.reshape(frames, rows, half_feat).astype(out_ref.dtype)

    n_keys = (2 * cols + 1) * C

    def attend(branch, c, at):
        r0 = pl.multiple_of(c * C, C)
        for p in range(feat // PAIR):
            sl = pl.ds(p * PAIR, PAIR)
            att[pl.ds(at, C), sl] = attend_pair(
                q[branch, pl.ds(r0, C), sl],
                kv[branch, pl.ds(r0, n_keys), sl],
                kv[branch, pl.ds(r0, n_keys), pl.ds(feat + p * PAIR, PAIR)],
            )

    def wait_halo(branch, g, side):
        halo(branch, g, side, g * G).wait_recv()

    @pl.when(is_cond)
    def _():
        for g in range(groups):
            wait_halo(CTRL, g, 0)

        @pl.loop(0, groups)
        def _(j):
            wait_halo(CTRL, j, 1)
            for c in range(GROUP):
                attend(CTRL, j * GROUP + c, c * C)
            for d in range(n_head):
                part[j, d] = jnp.dot(att[...], wo[CTRL, d], preferred_element_type=F32).astype(BF16)
            stage1(j, 0).start()
            stage1(j, 1).start()

            @pl.when(j >= 1)
            def _():
                relay(j - 1)

            @pl.when(j >= 2)
            def _():
                collect(j - 2)

    for g in range(groups):
        wait_halo(BASE, g, 0)

    @pl.loop(0, cols)
    def _(c):
        @pl.when(lax.rem(c, GROUP) == 0)
        def _():
            wait_halo(BASE, lax.div(c, GROUP), 1)

        @pl.when(jnp.logical_and(is_cond, c == 1))
        def _():
            relay(groups - 1)
            collect(groups - 2)

        @pl.when(jnp.logical_and(is_cond, c == 3))
        def _():
            collect(groups - 1)

        attend(BASE, c, 0)
        for k in (2, 1, 3, 0):
            d = heads[k]
            val = jnp.dot(att[pl.ds(0, C), :], wo[BASE, d], preferred_element_type=F32)
            if k == 0:
                val += xg[head, :, c].reshape(C, feat).astype(F32)
            res = csum[lax.div(c, GROUP), pl.ds(pl.multiple_of(lax.rem(c, GROUP) * C, C), C), :]
            val += jnp.dot(res, wo[2, d], preferred_element_type=F32)
            val *= factor
            low, high = val[:, :half_feat], val[:, half_feat:]
            if k == 0:
                kept[c] = jnp.where(is_cond, low, high)
                give[c, 0, 1 - cfg] = jnp.where(is_cond, high, low).astype(BF16)
                final(c, 0, 1 - cfg).start()
            else:
                give[c, k, 0] = low.astype(BF16)
                give[c, k, 1] = high.astype(BF16)
                final(c, k, 0).start()
                final(c, k, 1).start()

        @pl.when(jnp.logical_and(is_cond, c >= 2))
        def _():
            finish(c - 2)

    @pl.loop(jnp.where(is_cond, cols - 2, 0), cols)
    def _(c):
        finish(c)

    for c in range(cols):
        own_send(c, 0, to_hp).wait_send()
        own_send(c, 1, to_hm).wait_send()
        gather(hm, c, 2, to_hp).wait_send()

    for g in range(groups):
        for side in range(2):
            halo(BASE, g, side, g * G).wait_send()

    @pl.when(is_cond)
    def _():
        for g in range(groups):
            for side in range(2):
                halo(CTRL, g, side, g * G).wait_send()
                stage1(g, side).wait_send()
                stage2(g, side).wait_send()

    @pl.loop(0, cols)
    def _(c):
        for k in range(1, n_head):
            for side in range(2):
                final(c, k, side).wait_send()
        final(c, 0, 1 - cfg).wait_send()


def local(
    latents,
    timestep,
    guide_num,
    guide_den,
    depth_level,
    depth_table,
    time_weight,
    base_q,
    base_k,
    base_v,
    base_o,
    ctrl_q,
    ctrl_k,
    ctrl_v,
    ctrl_o,
    zero_linear,
):
    x = latents[0].transpose(0, 2, 1, 3)
    frames, cols, rows, feat = x.shape
    n_lon, n_head = lax.axis_size("lon"), lax.axis_size("head")
    C, T, width = frames * rows, frames * rows * cols, feat * n_head
    freqs = jnp.exp(-math.log(10000.0) * jnp.arange(FREQ // 2).astype(F32) / (FREQ // 2))
    freqs = jnp.broadcast_to(freqs[None, :], (16, FREQ // 2))
    dma = pltpu.SemaphoreType.DMA
    vmem = pl.BlockSpec(memory_space=pltpu.VMEM)
    smem = pl.BlockSpec(memory_space=pltpu.SMEM)
    hbm = pl.BlockSpec(memory_space=pl.ANY)
    groups = cols // GROUP
    out = pl.pallas_call(
        functools.partial(kernel, (frames, rows, cols, feat, n_lon, n_head)),
        out_shape=jax.ShapeDtypeStruct((frames, cols, rows, feat // 2), BF16),
        in_specs=[hbm, smem, smem, smem, vmem, vmem, vmem] + [hbm] * 10,
        out_specs=vmem,
        scratch_shapes=[
            pltpu.VMEM((n_head, frames, cols, rows, feat), BF16),
            pltpu.VMEM((FREQ, 2 * width), BF16),
            pltpu.VMEM((2, width, 3 * feat), BF16),
            pltpu.VMEM((3, n_head, feat, feat), BF16),
            pltpu.VMEM((16, 2 * width), F32),
            pltpu.VMEM((2, GROUP * C, width), BF16),
            pltpu.VMEM((2, T, feat), BF16),
            pltpu.VMEM((2, 3 * T, 2 * feat), BF16),
            pltpu.VMEM((GROUP * C, feat), BF16),
            pltpu.VMEM((groups, GROUP * C, feat), BF16),
            pltpu.VMEM((groups, n_head, GROUP * C, feat), BF16),
            pltpu.VMEM((groups, 2, C, feat), BF16),
            pltpu.VMEM((groups, 2, GROUP * C, feat), BF16),
            pltpu.VMEM((cols, C, feat // 2), F32),
            pltpu.VMEM((cols, n_head, 2, C, feat // 2), BF16),
            pltpu.VMEM((cols, n_head, 2, C, feat // 2), BF16),
            dma((20,)),
            dma((3, cols)),
            dma((3, cols)),
            dma((2, groups, 2)),
            dma((2, groups, 2)),
            dma((groups, 2)),
            dma((groups, 2)),
            dma((groups, 2)),
            dma((groups, 2)),
            dma((cols, n_head, 2)),
            dma((cols, n_head, 2)),
        ],
        compiler_params=pltpu.CompilerParams(
            collective_id=0, has_side_effects=True, vmem_limit_bytes=58 * 1024 * 1024
        ),
    )(
        x,
        timestep,
        guide_num,
        guide_den,
        depth_level.transpose(2, 0, 1),
        freqs,
        depth_table,
        time_weight,
        base_q,
        base_k,
        base_v,
        base_o,
        ctrl_q,
        ctrl_k,
        ctrl_v,
        ctrl_o,
        zero_linear,
    )
    return out.transpose(0, 2, 1, 3)


def solution(mesh):
    return jax.shard_map(
        local,
        mesh=mesh,
        in_specs=(
            P("cfg", None, None, "lon", "head"),
            P(),
            P(),
            P(),
            P(None, None, "lon"),
            P(),
            P(),
            P(None, "head"),
            P(None, "head"),
            P(None, "head"),
            P("head", None),
            P(None, "head"),
            P(None, "head"),
            P(None, "head"),
            P("head", None),
            P("head", None),
        ),
        out_specs=P(None, None, "lon", ("head", "cfg")),
        check_vma=False,
    )
```

time: 92.6 us -> 92 us (level); the launches traced: 91 us -> 91.8 us
  Pallas kernels: 85 us -> 87.5 us
    pallas_call x1, Pallas kernels: 85 us -> 87.5 us  [local(): pl.pallas_call(functools.partial(kernel, (frames, rows, cols, feat, n_lon...]
where the time goes in v1:
time: 92 us; the launch traced here: 91.8 us
  Pallas kernels  87.5 us (95%)
  local copies, waits for them, and re-layouts  2.3 us (2%)
  between operations  1.96 us (2%)
    pallas_call x1, Pallas kernels, local(): pl.pallas_call(functools.partial(kernel, (frames, rows, cols, feat, n_lon...  87.5 us

profile of v1, /device:TPU:4, one launch (start us, length us, event | category | flops | bytes accessed | tf_op | source)
XLA Modules:
  0.0 91.8 jit_solution(3133917903579716772)
XLA Ops:
  2.0 0.6 broadcast_in_dim.2.freq_ref
  2.6 87.5 %shard_map.154 = bf16[2,6,48,192]{3,2,1,0:T(8,128)(2,1)} custom-call(bf16[2,6,48,384]{3,2,1,0:T(8,128)(2,1)} %bitcast.6, s32[1]{0:T(128)S(6)} %copy.18.step_ref, s32[1]{0:T(128)S(6)} %copy.19.num_ref, s32[1]{0:T(128)S(6)} %copy.20.den_ref, s32[6,2,48]{2,1,0:T(2,128)} %bitcast.7, f32[16,128]{1,0:T(8,128)} %broadcast_in_dim.2.freq_ref, ...), custom_call_target="tpu_custom_call" | custom-call | tf_op jit(solution)/shard_map/pallas_call | solution.py:415
  90.1 1.7 %copy.21 = bf16[2,48,6,192]{3,1,2,0:T(8,128)(2,1)} copy(bf16[2,48,6,192]{3,1,2,0:T(8,128)(2,1)} %bitcast.5) | data formatting | bytes 442368
  (1 shorter events, 0.0 us)

commit v2 on v1

--- a/solution.py
+++ b/solution.py
@@ -63,22 +63,23 @@
     att,
     csum,
     part,
-    r1,
-    r2,
-    kept,
+    parts_in,
     give,
     take,
+    mine,
+    swap_out,
+    swap_in,
     load_sem,
     g_send,
     g_recv,
     h_send,
     h_recv,
-    s1_send,
-    s1_recv,
-    s2_send,
-    s2_recv,
+    p_send,
+    p_recv,
     f_send,
     f_recv,
+    x_send,
+    x_recv,
 ):
     frames, rows, cols, feat, n_lon, n_head = dims
     C = frames * rows
@@ -88,12 +89,12 @@
     G = GROUP * C
     lon, head, cfg = lax.axis_index("lon"), lax.axis_index("head"), lax.axis_index("cfg")
     is_cond = cfg == 0
-    hp, hm, ho = lax.rem(head + 1, n_head), lax.rem(head + n_head - 1, n_head), lax.rem(head + 2, n_head)
     lp, lm = lax.rem(lon + 1, n_lon), lax.rem(lon + n_lon - 1, n_lon)
-    to_hp, to_hm = (lon, hp, cfg), (lon, hm, cfg)
     to_lp, to_lm = (lp, head, cfg), (lm, head, cfg)
     half_feat = feat // 2
-    heads = [head, hp, ho, hm]
+    heads = [head] + [lax.rem(head + k, n_head) for k in range(1, n_head)]
+    peers = range(1, n_head)
+    to_cfg = (lon, head, 1 - cfg)
 
     own_copy = pltpu.make_async_copy(x_hbm, xg.at[head], load_sem.at[0])
     own_copy.start()
@@ -111,38 +112,28 @@
     loads = [pltpu.make_async_copy(s, d, load_sem.at[i + 1]) for i, (s, d) in enumerate(loads)]
 
     barrier = pltpu.get_barrier_semaphore()
-    group = [(lon, h, cfg) for h in heads[1:]] + [(lon, h, 1 - cfg) for h in heads]
-    for who in group + [to_lp, to_lm]:
+    partners = [(lon, heads[k], cfg) for k in peers] + [to_cfg, to_lp, to_lm]
+    for who in partners:
         pl.semaphore_signal(barrier, inc=1, device_id=who, device_id_type=MESH)
     for copy in loads:
         copy.start()
-    pl.semaphore_wait(barrier, len(group) + 2)
+    pl.semaphore_wait(barrier, len(partners))
 
     def send(src, dst, ssem, rsem, who):
         return pltpu.make_async_remote_copy(
             src_ref=src, dst_ref=dst, send_sem=ssem, recv_sem=rsem, device_id=who, device_id_type=MESH
         )
 
-    def gather(slot, c, kind, who):
-        place = xg.at[slot, :, c]
-        return send(place, place, g_send.at[kind, c], g_recv.at[kind, c], who)
-
-    def own_send(c, kind, who):
-        return send(x_hbm.at[:, c], xg.at[head, :, c], g_send.at[kind, c], g_recv.at[kind, c], who)
-
-    def own_sends(c):
-        own_send(c, 0, to_hp).start()
-        own_send(c, 1, to_hm).start()
-
-    def serve(c):
-        gather(hm, c, 0, to_hp).wait_recv()
-        gather(hp, c, 1, to_hm).wait_recv()
-        if c % 2 == 0:
-            gather(hm, c, 2, to_hp).start()
-        else:
-            gather(hp, c, 2, to_hm).start()
-        if c + 3 < cols:
-            own_sends(c + 3)
+    def to_peer(src, dst, ssem, rsem, k):
+        return send(src, dst, ssem, rsem, (lon, heads[k], cfg))
+
+    def gather(c, k):
+        return to_peer(
+            x_hbm.at[:, c], xg.at[head, :, c], g_send.at[k, c], g_recv.at[n_head - k, c], k
+        )
+
+    def gathered(c, k):
+        return to_peer(x_hbm.at[:, c], xg.at[heads[k], :, c], g_send.at[k, c], g_recv.at[k, c], k)
 
     def halo(branch, g, side, row0):
         src = kv.at[branch, pl.ds(T + row0, G)]
@@ -182,8 +173,9 @@
             normed, wqkv[branch, :, feat:], preferred_element_type=F32
         ).astype(BF16)
 
-    for c in range(3):
-        own_sends(c)
+    for c in range(cols):
+        for k in (2, 1, 3):
+            gather(c, k).start()
 
     @pl.when(jnp.logical_not(is_cond))
     def _():
@@ -200,14 +192,10 @@
     for copy in loads[1:]:
         copy.wait()
 
-    served = 0
     for g in range(groups):
-        until = min(cols, (g + 2) * GROUP)
-        for c in range(served, until):
-            serve(c)
-        served = until
         for c in range(g * GROUP, (g + 1) * GROUP):
-            gather(ho, c, 2, to_hp).wait_recv()
+            for k in peers:
+                gathered(c, k).wait_recv()
 
         @pl.when(is_cond)
         def _():
@@ -228,50 +216,45 @@
             for side in range(2):
                 halo(BASE, g, side, g * G).start()
 
-    def stage1(j, way):
-        src = part.at[j, ho, pl.ds(way * C, C)]
-        return send(src, r1.at[j, way], s1_send.at[j, way], s1_recv.at[j, way], to_hp if way == 0 else to_hm)
-
-    def stage2(j, way):
-        src = part.at[j, hp if way == 0 else hm]
-        return send(src, r2.at[j, way], s2_send.at[j, way], s2_recv.at[j, way], to_hp if way == 0 else to_hm)
-
-    def relay(j):
-        for way, d in ((0, hp), (1, hm)):
-            stage1(j, way).wait_recv()
-            sl = pl.ds(way * C, C)
-            part[j, d, sl] = (part[j, d, sl].astype(F32) + r1[j, way].astype(F32)).astype(BF16)
-            stage2(j, way).start()
+    def ctrl_sum(j, k):
+        return to_peer(part.at[j, k], parts_in.at[j, n_head - k], p_send.at[j, k], p_recv.at[j, n_head - k], k)
+
+    def ctrl_in(j, k):
+        return to_peer(part.at[j, k], parts_in.at[j, k], p_send.at[j, k], p_recv.at[j, k], k)
 
     def collect(j):
-        stage2(j, 0).wait_recv()
-        stage2(j, 1).wait_recv()
-        total = part[j, head].astype(F32) + r2[j, 0].astype(F32) + r2[j, 1].astype(F32)
+        total = part[j, 0].astype(F32)
+        for k in peers:
+            ctrl_in(j, k).wait_recv()
+            total = total + parts_in[j, k].astype(F32)
         csum[j] = total.astype(BF16)
 
-    def final(c, k, side):
-        there = (n_head - k) % n_head
-        return send(
-            give.at[c, k, side],
-            take.at[c, there, cfg],
-            f_send.at[c, k, side],
-            f_recv.at[c, there, cfg],
-            (lon, heads[k], side),
-        )
-
-    def final_in(c, k, side):
-        return send(
-            give.at[c, k, side], take.at[c, k, side], f_send.at[c, k, side], f_recv.at[c, k, side], to_hp
-        )
+    def base_sum(c, k):
+        return to_peer(give.at[c, k], take.at[c, n_head - k], f_send.at[c, k], f_recv.at[c, n_head - k], k)
+
+    def base_in(c, k):
+        return to_peer(give.at[c, k], take.at[c, k], f_send.at[c, k], f_recv.at[c, k], k)
+
+    def swap(c):
+        return send(swap_out.at[c], swap_in.at[c], x_send.at[c], x_recv.at[c], to_cfg)
+
+    def reduce(c):
+        total = give[c, 0].astype(F32) + xg[head, :, c].reshape(C, feat).astype(F32)
+        for k in peers:
+            base_in(c, k).wait_recv()
+            total = total + take[c, k].astype(F32)
+        total = total * factor
+        low, high = total[:, :half_feat], total[:, half_feat:]
+        mine[c] = jnp.where(is_cond, low, high)
+        other = jnp.where(is_cond, high, low).astype(BF16)
+        swap_out[c] = jnp.concatenate([other[: C // 2], other[C // 2 :]], axis=1)
+        swap(c).start()
 
     def finish(c):
-        total = kept[c]
-        for k in range(1, n_head):
-            for side in range(2):
-                final_in(c, k, side).wait_recv()
-                total = total + take[c, k, side].astype(F32)
-        final_in(c, 0, 1 - cfg).wait_recv()
-        total = total + take[c, 0, 1 - cfg].astype(F32)
+        swap(c).wait_recv()
+        other = swap_in[c]
+        other = jnp.concatenate([other[:, :half_feat], other[:, half_feat:]], axis=0)
+        total = mine[c] + other.astype(F32)
         out_ref[:, c] = total.reshape(frames, rows, half_feat).astype(out_ref.dtype)
 
     n_keys = (2 * cols + 1) * C
@@ -299,18 +282,15 @@
             wait_halo(CTRL, j, 1)
             for c in range(GROUP):
                 attend(CTRL, j * GROUP + c, c * C)
-            for d in range(n_head):
-                part[j, d] = jnp.dot(att[...], wo[CTRL, d], preferred_element_type=F32).astype(BF16)
-            stage1(j, 0).start()
-            stage1(j, 1).start()
+            for k in (2, 1, 3, 0):
+                val = jnp.dot(att[...], wo[CTRL, heads[k]], preferred_element_type=F32)
+                part[j, k] = val.astype(BF16)
+                if k:
+                    ctrl_sum(j, k).start()
 
             @pl.when(j >= 1)
             def _():
-                relay(j - 1)
-
-            @pl.when(j >= 2)
-            def _():
-                collect(j - 2)
+                collect(j - 1)
 
     for g in range(groups):
         wait_halo(BASE, g, 0)
@@ -321,47 +301,34 @@
         def _():
             wait_halo(BASE, lax.div(c, GROUP), 1)
 
-        @pl.when(jnp.logical_and(is_cond, c == 1))
-        def _():
-            relay(groups - 1)
-            collect(groups - 2)
-
         @pl.when(jnp.logical_and(is_cond, c == 3))
         def _():
             collect(groups - 1)
 
         attend(BASE, c, 0)
+        res = csum[lax.div(c, GROUP), pl.ds(pl.multiple_of(lax.rem(c, GROUP) * C, C), C), :]
         for k in (2, 1, 3, 0):
             d = heads[k]
             val = jnp.dot(att[pl.ds(0, C), :], wo[BASE, d], preferred_element_type=F32)
-            if k == 0:
-                val += xg[head, :, c].reshape(C, feat).astype(F32)
-            res = csum[lax.div(c, GROUP), pl.ds(pl.multiple_of(lax.rem(c, GROUP) * C, C), C), :]
             val += jnp.dot(res, wo[2, d], preferred_element_type=F32)
-            val *= factor
-            low, high = val[:, :half_feat], val[:, half_feat:]
-            if k == 0:
-                kept[c] = jnp.where(is_cond, low, high)
-                give[c, 0, 1 - cfg] = jnp.where(is_cond, high, low).astype(BF16)
-                final(c, 0, 1 - cfg).start()
-            else:
-                give[c, k, 0] = low.astype(BF16)
-                give[c, k, 1] = high.astype(BF16)
-                final(c, k, 0).start()
-                final(c, k, 1).start()
-
-        @pl.when(jnp.logical_and(is_cond, c >= 2))
+            give[c, k] = val.astype(BF16)
+            if k:
+                base_sum(c, k).start()
+
+        @pl.when(c >= 2)
         def _():
-            finish(c - 2)
-
-    @pl.loop(jnp.where(is_cond, cols - 2, 0), cols)
+            reduce(c - 2)
+
+    reduce(cols - 2)
+    reduce(cols - 1)
+
+    @pl.loop(0, cols)
     def _(c):
         finish(c)
 
     for c in range(cols):
-        own_send(c, 0, to_hp).wait_send()
-        own_send(c, 1, to_hm).wait_send()
-        gather(hm, c, 2, to_hp).wait_send()
+        for k in peers:
+            gather(c, k).wait_send()
 
     for g in range(groups):
         for side in range(2):
@@ -372,15 +339,14 @@
         for g in range(groups):
             for side in range(2):
                 halo(CTRL, g, side, g * G).wait_send()
-                stage1(g, side).wait_send()
-                stage2(g, side).wait_send()
+            for k in peers:
+                ctrl_sum(g, k).wait_send()
 
     @pl.loop(0, cols)
     def _(c):
-        for k in range(1, n_head):
-            for side in range(2):
-                final(c, k, side).wait_send()
-        final(c, 0, 1 - cfg).wait_send()
+        for k in peers:
+            base_sum(c, k).wait_send()
+        swap(c).wait_send()
 
 
 def local(
@@ -429,22 +395,23 @@
             pltpu.VMEM((GROUP * C, feat), BF16),
             pltpu.VMEM((groups, GROUP * C, feat), BF16),
             pltpu.VMEM((groups, n_head, GROUP * C, feat), BF16),
-            pltpu.VMEM((groups, 2, C, feat), BF16),
-            pltpu.VMEM((groups, 2, GROUP * C, feat), BF16),
+            pltpu.VMEM((groups, n_head, GROUP * C, feat), BF16),
+            pltpu.VMEM((cols, n_head, C, feat), BF16),
+            pltpu.VMEM((cols, n_head, C, feat), BF16),
             pltpu.VMEM((cols, C, feat // 2), F32),
-            pltpu.VMEM((cols, n_head, 2, C, feat // 2), BF16),
-            pltpu.VMEM((cols, n_head, 2, C, feat // 2), BF16),
+            pltpu.VMEM((cols, C // 2, feat), BF16),
+            pltpu.VMEM((cols, C // 2, feat), BF16),
             dma((20,)),
-            dma((3, cols)),
-            dma((3, cols)),
+            dma((n_head, cols)),
+            dma((n_head, cols)),
             dma((2, groups, 2)),
             dma((2, groups, 2)),
-            dma((groups, 2)),
-            dma((groups, 2)),
-            dma((groups, 2)),
-            dma((groups, 2)),
-            dma((cols, n_head, 2)),
-            dma((cols, n_head, 2)),
+            dma((groups, n_head)),
+            dma((groups, n_head)),
+            dma((cols, n_head)),
+            dma((cols, n_head)),
+            dma((cols,)),
+            dma((cols,)),
         ],
         compiler_params=pltpu.CompilerParams(
             collective_id=0, has_side_effects=True, vmem_limit_bytes=58 * 1024 * 1024

time: 92 us -> 88.8 us (0.965)
  Pallas kernels: 87.5 us -> 84.3 us
    pallas_call x1, Pallas kernels: 87.5 us -> 84.3 us  [local(): pl.pallas_call(functools.partial(kernel, (frames, rows, cols, feat, n_lon...]
where the time goes in v2:
time: 88.8 us; the launch traced here: 88.5 us
  Pallas kernels  84.3 us (95%)
  local copies, waits for them, and re-layouts  2.3 us (3%)
  between operations  1.96 us (2%)
    pallas_call x1, Pallas kernels, local(): pl.pallas_call(functools.partial(kernel, (frames, rows, cols, feat, n_lon...  84.3 us

profile of v2, /device:TPU:4, one launch (start us, length us, event | category | flops | bytes accessed | tf_op | source)
XLA Modules:
  0.0 88.5 jit_solution(17187103441912482542)
XLA Ops:
  2.0 0.6 broadcast_in_dim.2.freq_ref
  2.6 84.3 %shard_map.154 = bf16[2,6,48,192]{3,2,1,0:T(8,128)(2,1)} custom-call(bf16[2,6,48,384]{3,2,1,0:T(8,128)(2,1)} %bitcast.6, s32[1]{0:T(128)S(6)} %copy.18.step_ref, s32[1]{0:T(128)S(6)} %copy.19.num_ref, s32[1]{0:T(128)S(6)} %copy.20.den_ref, s32[6,2,48]{2,1,0:T(2,128)} %bitcast.7, f32[16,128]{1,0:T(8,128)} %broadcast_in_dim.2.freq_ref, ...), custom_call_target="tpu_custom_call" | custom-call | tf_op jit(solution)/shard_map/pallas_call | solution.py:381
  86.8 1.7 %copy.21 = bf16[2,48,6,192]{3,1,2,0:T(8,128)(2,1)} copy(bf16[2,48,6,192]{3,1,2,0:T(8,128)(2,1)} %bitcast.5) | data formatting | bytes 442368
  (1 shorter events, 0.0 us)

commit v3 on v2

--- a/solution.py
+++ b/solution.py
@@ -18,16 +18,41 @@
 MESH = pl.DeviceIdType.MESH
 
 
-def attend_pair(q, k, v):
+def attend_pair(q, k, v, count, near):
     rows = q.shape[0]
+    C = rows // count
+    total = k.shape[0]
     low = lax.broadcasted_iota(jnp.int32, (rows, PAIR), 1) < HD
     zero = jnp.zeros_like(q)
     both = jnp.concatenate([jnp.where(low, q, zero), jnp.where(low, zero, q)], axis=0)
     scores = lax.dot_general(both, k, (((1,), (1,)), ((), ())), preferred_element_type=F32)
-    top = jnp.max(scores, axis=1, keepdims=True)
-    expo = jnp.exp2(scores - top).astype(BF16)
+    lane = lax.broadcasted_iota(jnp.int32, (C, 128), 1)
+    weights = []
+    for h in range(2):
+        for b in range(count):
+            r0 = (count * h + b) * C
+            first, last = b * C, (b + near) * C
+            t0, t1 = first // 128, -(-last // 128)
+            tiles = []
+            for t in range(t0, t1):
+                at, end = t * 128, min(t * 128 + 128, total)
+                tile = scores[r0 : r0 + C, at:end]
+                if at < first:
+                    tile = jnp.where(lane[:, : end - at] >= first - at, tile, -1e30)
+                if end > last:
+                    tile = jnp.where(lane[:, : end - at] < last - at, tile, -1e30)
+                tiles.append(tile)
+            row = jnp.concatenate(tiles, axis=1)
+            top = jnp.max(row, axis=1, keepdims=True)
+            expo = [jnp.exp2(row - top).astype(BF16)]
+            if t0:
+                expo = [jnp.zeros((C, t0 * 128), BF16)] + expo
+            if t1 * 128 < total:
+                expo = expo + [jnp.zeros((C, total - t1 * 128), BF16)]
+            weights.append(jnp.concatenate(expo, axis=1) if len(expo) > 1 else expo[0])
+    weights = jnp.concatenate(weights, axis=0)
     ones = jnp.concatenate([v, jnp.ones_like(v)], axis=1)
-    mixed = jnp.dot(expo, ones, preferred_element_type=F32)
+    mixed = jnp.dot(weights, ones, preferred_element_type=F32)
     mixed = mixed[:, :PAIR] / mixed[:, PAIR:]
     return jnp.where(low, mixed[:rows], mixed[rows:]).astype(BF16)
 
@@ -257,16 +282,19 @@
         total = mine[c] + other.astype(F32)
         out_ref[:, c] = total.reshape(frames, rows, half_feat).astype(out_ref.dtype)
 
-    n_keys = (2 * cols + 1) * C
-
-    def attend(branch, c, at):
-        r0 = pl.multiple_of(c * C, C)
+    near = 2 * cols + 1
+    n_keys = (near + GROUP - 1) * C
+
+    def attend(branch, j):
+        r0 = j * G
         for p in range(feat // PAIR):
             sl = pl.ds(p * PAIR, PAIR)
-            att[pl.ds(at, C), sl] = attend_pair(
-                q[branch, pl.ds(r0, C), sl],
+            att[:, sl] = attend_pair(
+                q[branch, pl.ds(r0, G), sl],
                 kv[branch, pl.ds(r0, n_keys), sl],
                 kv[branch, pl.ds(r0, n_keys), pl.ds(feat + p * PAIR, PAIR)],
+                GROUP,
+                near,
             )
 
     def wait_halo(branch, g, side):
@@ -277,50 +305,46 @@
         for g in range(groups):
             wait_halo(CTRL, g, 0)
 
-        @pl.loop(0, groups)
-        def _(j):
+        for j in range(groups):
             wait_halo(CTRL, j, 1)
-            for c in range(GROUP):
-                attend(CTRL, j * GROUP + c, c * C)
+            attend(CTRL, j)
             for k in (2, 1, 3, 0):
                 val = jnp.dot(att[...], wo[CTRL, heads[k]], preferred_element_type=F32)
                 part[j, k] = val.astype(BF16)
                 if k:
                     ctrl_sum(j, k).start()
-
-            @pl.when(j >= 1)
-            def _():
+            if j >= 1:
                 collect(j - 1)
 
     for g in range(groups):
         wait_halo(BASE, g, 0)
 
-    @pl.loop(0, cols)
-    def _(c):
-        @pl.when(lax.rem(c, GROUP) == 0)
-        def _():
-            wait_halo(BASE, lax.div(c, GROUP), 1)
-
-        @pl.when(jnp.logical_and(is_cond, c == 3))
-        def _():
-            collect(groups - 1)
-
-        attend(BASE, c, 0)
-        res = csum[lax.div(c, GROUP), pl.ds(pl.multiple_of(lax.rem(c, GROUP) * C, C), C), :]
+    for j in range(groups):
+        wait_halo(BASE, j, 1)
+        attend(BASE, j)
+
+        if j == groups - 1:
+
+            @pl.when(is_cond)
+            def _():
+                collect(groups - 1)
+
         for k in (2, 1, 3, 0):
             d = heads[k]
-            val = jnp.dot(att[pl.ds(0, C), :], wo[BASE, d], preferred_element_type=F32)
-            val += jnp.dot(res, wo[2, d], preferred_element_type=F32)
-            give[c, k] = val.astype(BF16)
-            if k:
-                base_sum(c, k).start()
-
-        @pl.when(c >= 2)
-        def _():
-            reduce(c - 2)
-
-    reduce(cols - 2)
-    reduce(cols - 1)
+            val = jnp.dot(att[...], wo[BASE, d], preferred_element_type=F32)
+            val += jnp.dot(csum[j], wo[2, d], preferred_element_type=F32)
+            for b in range(GROUP):
+                c = j * GROUP + b
+                give[c, k] = val[b * C : (b + 1) * C].astype(BF16)
+                if k:
+                    base_sum(c, k).start()
+
+        if j >= 1:
+            for b in range(GROUP):
+                reduce((j - 1) * GROUP + b)
+
+    for b in range(GROUP):
+        reduce(cols - GROUP + b)
 
     @pl.loop(0, cols)
     def _(c):

time: 88.8 us -> 87.5 us (0.985)
  Pallas kernels: 84.3 us -> 83 us
    pallas_call x1, Pallas kernels: 84.3 us -> 83 us  [local(): pl.pallas_call(functools.partial(kernel, (frames, rows, cols, feat, n_lon...]
where the time goes in v3:
time: 87.5 us; the launch traced here: 87.3 us
  Pallas kernels  83 us (95%)
  local copies, waits for them, and re-layouts  2.3 us (3%)
  between operations  1.96 us (2%)
    pallas_call x1, Pallas kernels, local(): pl.pallas_call(functools.partial(kernel, (frames, rows, cols, feat, n_lon...  83 us

profile of v3, /device:TPU:4, one launch (start us, length us, event | category | flops | bytes accessed | tf_op | source)
XLA Modules:
  0.0 87.3 jit_solution(16443445275850328685)
XLA Ops:
  2.0 0.6 broadcast_in_dim.2.freq_ref
  2.6 83.0 %shard_map.154 = bf16[2,6,48,192]{3,2,1,0:T(8,128)(2,1)} custom-call(bf16[2,6,48,384]{3,2,1,0:T(8,128)(2,1)} %bitcast.6, s32[1]{0:T(128)S(6)} %copy.18.step_ref, s32[1]{0:T(128)S(6)} %copy.19.num_ref, s32[1]{0:T(128)S(6)} %copy.20.den_ref, s32[6,2,48]{2,1,0:T(2,128)} %bitcast.7, f32[16,128]{1,0:T(8,128)} %broadcast_in_dim.2.freq_ref, ...), custom_call_target="tpu_custom_call" | custom-call | tf_op jit(solution)/shard_map/pallas_call | solution.py:405
  85.6 1.7 %copy.21 = bf16[2,48,6,192]{3,1,2,0:T(8,128)(2,1)} copy(bf16[2,48,6,192]{3,1,2,0:T(8,128)(2,1)} %bitcast.5) | data formatting | bytes 442368
  (1 shorter events, 0.0 us)

commit v4 on v3

--- a/solution.py
+++ b/solution.py
@@ -117,6 +117,10 @@
     lp, lm = lax.rem(lon + 1, n_lon), lax.rem(lon + n_lon - 1, n_lon)
     to_lp, to_lm = (lp, head, cfg), (lm, head, cfg)
     half_feat = feat // 2
+    core = lax.rem(lon, 2)
+    make = [jnp.where(core == 0, g, groups - 1 - g) for g in range(groups)]
+    order = [jnp.where(core == 0, groups - 1 - g, g) for g in range(groups)]
+    make_cols = [jnp.where(core == 0, c, cols - 1 - c) for c in range(cols)]
     heads = [head] + [lax.rem(head + k, n_head) for k in range(1, n_head)]
     peers = range(1, n_head)
     to_cfg = (lon, head, 1 - cfg)
@@ -160,11 +164,21 @@
     def gathered(c, k):
         return to_peer(x_hbm.at[:, c], xg.at[heads[k], :, c], g_send.at[k, c], g_recv.at[k, c], k)
 
-    def halo(branch, g, side, row0):
-        src = kv.at[branch, pl.ds(T + row0, G)]
-        dst = kv.at[branch, pl.ds((0 if side == 0 else 2 * T) + row0, G)]
+    def own_rows(g):
+        return pl.ds(pl.multiple_of(T + g * G, G), G)
+
+    def halo(branch, g, side):
+        dst = pl.ds(pl.multiple_of((0 if side == 0 else 2 * T) + g * G, G), G)
         who = to_lp if side == 0 else to_lm
-        return send(src, dst, h_send.at[branch, g, side], h_recv.at[branch, g, side], who)
+        return send(
+            kv.at[branch, own_rows(g)], kv.at[branch, dst], h_send.at[branch, g, side], h_recv.at[branch, g, side], who
+        )
+
+    def wait_halo(branch, g, side):
+        dst = pl.ds(pl.multiple_of(2 * T * side + g * G, G), G)
+        send(
+            kv.at[branch, own_rows(g)], kv.at[branch, dst], h_send.at[branch, g, side], h_recv.at[branch, g, side], to_lp
+        ).wait_recv()
 
     def normalise(branch, c, at):
         parts = [xg[j, :, c].reshape(C, feat).astype(F32) for j in range(n_head)]
@@ -190,15 +204,16 @@
     def project(branch, g):
         for c in range(GROUP):
             normalise(branch, g * GROUP + c, c * C)
-        row0 = g * G
         normed = ms[branch]
-        query = jnp.dot(normed, wqkv[branch, :, :feat], preferred_element_type=F32)
-        q[branch, pl.ds(row0, G), :] = (query * (math.log2(math.e) / math.sqrt(HD))).astype(BF16)
-        kv[branch, pl.ds(T + row0, G), :] = jnp.dot(
+        kv[branch, own_rows(g), :] = jnp.dot(
             normed, wqkv[branch, :, feat:], preferred_element_type=F32
         ).astype(BF16)
-
-    for c in range(cols):
+        for side in range(2):
+            halo(branch, g, side).start()
+        query = jnp.dot(normed, wqkv[branch, :, :feat], preferred_element_type=F32)
+        q[branch, pl.ds(pl.multiple_of(g * G, G), G), :] = (query * (math.log2(math.e) / math.sqrt(HD))).astype(BF16)
+
+    for c in make_cols:
         for k in (2, 1, 3):
             gather(c, k).start()
 
@@ -217,29 +232,16 @@
     for copy in loads[1:]:
         copy.wait()
 
-    for g in range(groups):
-        for c in range(g * GROUP, (g + 1) * GROUP):
+    for i, g in enumerate(make):
+        for c in make_cols[i * GROUP : (i + 1) * GROUP]:
             for k in peers:
                 gathered(c, k).wait_recv()
 
         @pl.when(is_cond)
         def _():
             project(CTRL, g)
-            for side in range(2):
-                halo(CTRL, g, side, g * G).start()
 
         project(BASE, g)
-
-        @pl.when(jnp.logical_not(is_cond))
-        def _():
-            for side in range(2):
-                halo(BASE, g, side, g * G).start()
-
-    @pl.when(is_cond)
-    def _():
-        for g in range(groups):
-            for side in range(2):
-                halo(BASE, g, side, g * G).start()
 
     def ctrl_sum(j, k):
         return to_peer(part.at[j, k], parts_in.at[j, n_head - k], p_send.at[j, k], p_recv.at[j, n_head - k], k)
@@ -286,7 +288,7 @@
     n_keys = (near + GROUP - 1) * C
 
     def attend(branch, j):
-        r0 = j * G
+        r0 = pl.multiple_of(j * G, G)
         for p in range(feat // PAIR):
             sl = pl.ds(p * PAIR, PAIR)
             att[:, sl] = attend_pair(
@@ -297,37 +299,34 @@
                 near,
             )
 
-    def wait_halo(branch, g, side):
-        halo(branch, g, side, g * G).wait_recv()
-
     @pl.when(is_cond)
     def _():
         for g in range(groups):
-            wait_halo(CTRL, g, 0)
-
-        for j in range(groups):
-            wait_halo(CTRL, j, 1)
+            wait_halo(CTRL, g, 1 - core)
+
+        for j in order:
+            wait_halo(CTRL, j, core)
             attend(CTRL, j)
             for k in (2, 1, 3, 0):
                 val = jnp.dot(att[...], wo[CTRL, heads[k]], preferred_element_type=F32)
                 part[j, k] = val.astype(BF16)
                 if k:
                     ctrl_sum(j, k).start()
-            if j >= 1:
-                collect(j - 1)
 
     for g in range(groups):
-        wait_halo(BASE, g, 0)
-
-    for j in range(groups):
-        wait_halo(BASE, j, 1)
+        wait_halo(BASE, g, 1 - core)
+
+    def reduce_unit(j):
+        for b in range(GROUP):
+            reduce(j * GROUP + b)
+
+    for i, j in enumerate(order):
+        wait_halo(BASE, j, core)
         attend(BASE, j)
 
-        if j == groups - 1:
-
-            @pl.when(is_cond)
-            def _():
-                collect(groups - 1)
+        @pl.when(is_cond)
+        def _():
+            collect(j)
 
         for k in (2, 1, 3, 0):
             d = heads[k]
@@ -339,16 +338,15 @@
                 if k:
                     base_sum(c, k).start()
 
-        if j >= 1:
-            for b in range(GROUP):
-                reduce((j - 1) * GROUP + b)
-
-    for b in range(GROUP):
-        reduce(cols - GROUP + b)
-
-    @pl.loop(0, cols)
-    def _(c):
-        finish(c)
+        if i >= 2:
+            reduce_unit(order[i - 2])
+
+    for j in order[groups - 2 :]:
+        reduce_unit(j)
+
+    for j in order:
+        for b in range(GROUP):
+            finish(j * GROUP + b)
 
     for c in range(cols):
         for k in peers:
@@ -356,13 +354,13 @@
 
     for g in range(groups):
         for side in range(2):
-            halo(BASE, g, side, g * G).wait_send()
+            halo(BASE, g, side).wait_send()
 
     @pl.when(is_cond)
     def _():
         for g in range(groups):
             for side in range(2):
-                halo(CTRL, g, side, g * G).wait_send()
+                halo(CTRL, g, side).wait_send()
             for k in peers:
                 ctrl_sum(g, k).wait_send()
 

time: 87.5 us -> 83.8 us (0.958)
  the two profiles are of different devices: /device:TPU:4 before, /device:TPU:102 now
where the time goes in v4:
time: 83.8 us; the launch traced here: 83.6 us
  Pallas kernels  79.4 us (95%)
  local copies, waits for them, and re-layouts  2.3 us (3%)
  between operations  1.96 us (2%)
    pallas_call x1, Pallas kernels, local(): pl.pallas_call(functools.partial(kernel, (frames, rows, cols, feat, n_lon...  79.4 us
    unnamed x1, local copies, waits for them, and re-layouts  1.69 us

profile of v4, /device:TPU:102, one launch (start us, length us, event | category | flops | bytes accessed | tf_op | source)
XLA Modules:
  0.0 83.6 jit_solution(1855602646639238468)
XLA Ops:
  2.0 0.6 broadcast_in_dim.2.freq_ref
  2.6 79.4 %shard_map.154 = bf16[2,6,48,192]{3,2,1,0:T(8,128)(2,1)} custom-call(bf16[2,6,48,384]{3,2,1,0:T(8,128)(2,1)} %bitcast.6, s32[1]{0:T(128)S(6)} %copy.18.step_ref, s32[1]{0:T(128)S(6)} %copy.19.num_ref, s32[1]{0:T(128)S(6)} %copy.20.den_ref, s32[6,2,48]{2,1,0:T(2,128)} %bitcast.7, f32[16,128]{1,0:T(8,128)} %broadcast_in_dim.2.freq_ref, ...), custom_call_target="tpu_custom_call" | custom-call | tf_op jit(solution)/shard_map/pallas_call | solution.py:403
  81.9 1.7 %copy.21 = bf16[2,48,6,192]{3,1,2,0:T(8,128)(2,1)} copy(bf16[2,48,6,192]{3,1,2,0:T(8,128)(2,1)} %bitcast.5) | data formatting | bytes 442368
  (1 shorter events, 0.0 us)

commit v5 on v4

--- a/solution.py
+++ b/solution.py
@@ -86,12 +86,13 @@
     q,
     kv,
     att,
+    att_in,
+    x_in,
     csum,
     part,
     parts_in,
     give,
     take,
-    mine,
     swap_out,
     swap_in,
     load_sem,
@@ -99,6 +100,10 @@
     g_recv,
     h_send,
     h_recv,
+    a_send,
+    a_recv,
+    i_send,
+    i_recv,
     p_send,
     p_recv,
     f_send,
@@ -157,12 +162,25 @@
         return send(src, dst, ssem, rsem, (lon, heads[k], cfg))
 
     def gather(c, k):
-        return to_peer(
-            x_hbm.at[:, c], xg.at[head, :, c], g_send.at[k, c], g_recv.at[n_head - k, c], k
-        )
-
-    def gathered(c, k):
-        return to_peer(x_hbm.at[:, c], xg.at[heads[k], :, c], g_send.at[k, c], g_recv.at[k, c], k)
+        return to_peer(x_hbm.at[:, c], xg.at[head, :, c], g_send.at[k, c], g_recv.at[k, c], k)
+
+    def gathered(c, k, slot):
+        return to_peer(x_hbm.at[:, c], xg.at[heads[slot], :, c], g_send.at[k, c], g_recv.at[k, c], 1)
+
+    def relay(c, k):
+        place = xg.at[heads[4 - k], :, c]
+        return to_peer(place, place, g_send.at[2, c], g_recv.at[2, c], k)
+
+    def own_sends(i):
+        gather(make_cols[i], 1).start()
+        gather(make_cols[i], 3).start()
+
+    def serve(i):
+        gathered(make_cols[i], 1, 3).wait_recv()
+        gathered(make_cols[i], 3, 1).wait_recv()
+        relay(make_cols[i], 1 if i % 2 == 0 else 3).start()
+        if i + 3 < cols:
+            own_sends(i + 3)
 
     def own_rows(g):
         return pl.ds(pl.multiple_of(T + g * G, G), G)
@@ -213,13 +231,26 @@
         query = jnp.dot(normed, wqkv[branch, :, :feat], preferred_element_type=F32)
         q[branch, pl.ds(pl.multiple_of(g * G, G), G), :] = (query * (math.log2(math.e) / math.sqrt(HD))).astype(BF16)
 
-    for c in make_cols:
-        for k in (2, 1, 3):
-            gather(c, k).start()
-
-    @pl.when(jnp.logical_not(is_cond))
-    def _():
-        csum[...] = jnp.zeros_like(csum)
+    def my_col(j):
+        return j * GROUP + cfg
+
+    def other_col(j):
+        return j * GROUP + 1 - cfg
+
+    def col_rows(c):
+        return pl.ds(pl.multiple_of(c * C, C), C)
+
+    def share_x(j):
+        return send(x_hbm.at[:, other_col(j)], x_in.at[j], i_send.at[j], i_recv.at[j], to_cfg)
+
+    def share(branch, j):
+        src = att.at[branch, col_rows(other_col(j))]
+        return send(src, att_in.at[branch, j], a_send.at[branch, j], a_recv.at[branch, j], to_cfg)
+
+    for i in range(3):
+        own_sends(i)
+    for j in range(groups):
+        share_x(j).start()
 
     angles = freq_ref[...] * step_ref[0].astype(F32)
     temb = jnp.concatenate([jnp.cos(angles), jnp.sin(angles)], axis=1).astype(BF16)
@@ -227,15 +258,18 @@
     mod[...] = jnp.dot(temb, tw[...], preferred_element_type=F32)
     ones = jnp.ones((8, feat), F32)
     ratio = (ones * num_ref[0].astype(F32)) / (ones * den_ref[0].astype(F32))
-    factor = jnp.where(is_cond, ratio, 1.0 - ratio)[0:1, :]
+    ratio = ratio[0:1, :]
+    factor = jnp.where(is_cond, ratio, 1.0 - ratio)
     own_copy.wait()
     for copy in loads[1:]:
         copy.wait()
 
     for i, g in enumerate(make):
+        until = min(cols, (i + 2) * GROUP)
+        for n in range(0 if i == 0 else min(cols, (i + 1) * GROUP), until):
+            serve(n)
         for c in make_cols[i * GROUP : (i + 1) * GROUP]:
-            for k in peers:
-                gathered(c, k).wait_recv()
+            gathered(c, 2, 2).wait_recv()
 
         @pl.when(is_cond)
         def _():
@@ -256,33 +290,51 @@
             total = total + parts_in[j, k].astype(F32)
         csum[j] = total.astype(BF16)
 
-    def base_sum(c, k):
-        return to_peer(give.at[c, k], take.at[c, n_head - k], f_send.at[c, k], f_recv.at[c, n_head - k], k)
-
-    def base_in(c, k):
-        return to_peer(give.at[c, k], take.at[c, k], f_send.at[c, k], f_recv.at[c, k], k)
-
-    def swap(c):
-        return send(swap_out.at[c], swap_in.at[c], x_send.at[c], x_recv.at[c], to_cfg)
-
-    def reduce(c):
-        total = give[c, 0].astype(F32) + xg[head, :, c].reshape(C, feat).astype(F32)
+    def base_sum(j, k):
+        return to_peer(give.at[j, k], take.at[j, n_head - k], f_send.at[j, k], f_recv.at[j, n_head - k], k)
+
+    def base_in(j, k):
+        return to_peer(give.at[j, k], take.at[j, k], f_send.at[j, k], f_recv.at[j, k], k)
+
+    def swap(j):
+        return send(swap_out.at[j], swap_in.at[j], x_send.at[j], x_recv.at[j], to_cfg)
+
+    def ctrl_out(j, done):
+        for k in (2, 1, 3, 0):
+            part[j, k] = jnp.dot(done, wo[CTRL, heads[k]], preferred_element_type=F32).astype(BF16)
+            if k:
+                ctrl_sum(j, k).start()
+
+    def final_out(j):
+        own = att[BASE, col_rows(my_col(j)), :].astype(F32)
+        mixed = (own * factor + att_in[BASE, j].astype(F32) * (1.0 - factor)).astype(BF16)
+        for k in (2, 1, 3, 0):
+            d = heads[k]
+            val = jnp.dot(csum[j], wo[2, d], preferred_element_type=F32) * ratio
+            val += jnp.dot(mixed, wo[BASE, d], preferred_element_type=F32)
+            give[j, k] = val.astype(BF16)
+            if k:
+                base_sum(j, k).start()
+
+    def reduce(j):
+        c = my_col(j)
+        total = xg[head, :, c].reshape(C, feat).astype(F32) * factor
+        total = total + x_in[j].reshape(C, feat).astype(F32) * (1.0 - factor)
+        total = total + give[j, 0].astype(F32)
         for k in peers:
-            base_in(c, k).wait_recv()
-            total = total + take[c, k].astype(F32)
-        total = total * factor
+            base_in(j, k).wait_recv()
+            total = total + take[j, k].astype(F32)
         low, high = total[:, :half_feat], total[:, half_feat:]
-        mine[c] = jnp.where(is_cond, low, high)
         other = jnp.where(is_cond, high, low).astype(BF16)
-        swap_out[c] = jnp.concatenate([other[: C // 2], other[C // 2 :]], axis=1)
-        swap(c).start()
-
-    def finish(c):
-        swap(c).wait_recv()
-        other = swap_in[c]
+        swap_out[j] = jnp.concatenate([other[: C // 2], other[C // 2 :]], axis=1)
+        swap(j).start()
+        out_ref[:, c] = jnp.where(is_cond, low, high).astype(BF16).reshape(frames, rows, half_feat)
+
+    def finish(j):
+        swap(j).wait_recv()
+        other = swap_in[j]
         other = jnp.concatenate([other[:, :half_feat], other[:, half_feat:]], axis=0)
-        total = mine[c] + other.astype(F32)
-        out_ref[:, c] = total.reshape(frames, rows, half_feat).astype(out_ref.dtype)
+        out_ref[:, other_col(j)] = other.reshape(frames, rows, half_feat)
 
     near = 2 * cols + 1
     n_keys = (near + GROUP - 1) * C
@@ -291,66 +343,64 @@
         r0 = pl.multiple_of(j * G, G)
         for p in range(feat // PAIR):
             sl = pl.ds(p * PAIR, PAIR)
-            att[:, sl] = attend_pair(
+            att[branch, pl.ds(r0, G), sl] = attend_pair(
                 q[branch, pl.ds(r0, G), sl],
                 kv[branch, pl.ds(r0, n_keys), sl],
                 kv[branch, pl.ds(r0, n_keys), pl.ds(feat + p * PAIR, PAIR)],
                 GROUP,
                 near,
             )
+        share(branch, j).start()
+
+    first = jnp.where(is_cond, CTRL, BASE)
+    for g in range(groups):
+        wait_halo(first, g, 1 - core)
+
+    for j in order:
+        wait_halo(first, j, core)
+        attend(first, j)
+
+        @pl.when(is_cond)
+        def _():
+            ctrl_out(j, att[CTRL, col_rows(my_col(j)), :])
+
+    @pl.when(jnp.logical_not(is_cond))
+    def _():
+        for j in order:
+            share(CTRL, j).wait_recv()
+            ctrl_out(j, att_in[CTRL, j])
 
     @pl.when(is_cond)
     def _():
         for g in range(groups):
-            wait_halo(CTRL, g, 1 - core)
-
-        for j in order:
-            wait_halo(CTRL, j, core)
-            attend(CTRL, j)
-            for k in (2, 1, 3, 0):
-                val = jnp.dot(att[...], wo[CTRL, heads[k]], preferred_element_type=F32)
-                part[j, k] = val.astype(BF16)
-                if k:
-                    ctrl_sum(j, k).start()
-
-    for g in range(groups):
-        wait_halo(BASE, g, 1 - core)
-
-    def reduce_unit(j):
-        for b in range(GROUP):
-            reduce(j * GROUP + b)
+            wait_halo(BASE, g, 1 - core)
+
+    for j in range(groups):
+        share_x(j).wait_recv()
 
     for i, j in enumerate(order):
-        wait_halo(BASE, j, core)
-        attend(BASE, j)
 
         @pl.when(is_cond)
         def _():
-            collect(j)
-
-        for k in (2, 1, 3, 0):
-            d = heads[k]
-            val = jnp.dot(att[...], wo[BASE, d], preferred_element_type=F32)
-            val += jnp.dot(csum[j], wo[2, d], preferred_element_type=F32)
-            for b in range(GROUP):
-                c = j * GROUP + b
-                give[c, k] = val[b * C : (b + 1) * C].astype(BF16)
-                if k:
-                    base_sum(c, k).start()
-
+            wait_halo(BASE, j, core)
+            attend(BASE, j)
+
+        collect(j)
+        share(BASE, j).wait_recv()
+        final_out(j)
         if i >= 2:
-            reduce_unit(order[i - 2])
+            reduce(order[i - 2])
 
     for j in order[groups - 2 :]:
-        reduce_unit(j)
+        reduce(j)
 
     for j in order:
-        for b in range(GROUP):
-            finish(j * GROUP + b)
+        finish(j)
 
     for c in range(cols):
-        for k in peers:
-            gather(c, k).wait_send()
+        gather(c, 1).wait_send()
+        gather(c, 3).wait_send()
+        relay(c, 1).wait_send()
 
     for g in range(groups):
         for side in range(2):
@@ -361,14 +411,15 @@
         for g in range(groups):
             for side in range(2):
                 halo(CTRL, g, side).wait_send()
-            for k in peers:
-                ctrl_sum(g, k).wait_send()
-
-    @pl.loop(0, cols)
-    def _(c):
+            share(CTRL, g).wait_send()
+
+    for j in range(groups):
+        share_x(j).wait_send()
+        share(BASE, j).wait_send()
         for k in peers:
-            base_sum(c, k).wait_send()
-        swap(c).wait_send()
+            ctrl_sum(j, k).wait_send()
+            base_sum(j, k).wait_send()
+        swap(j).wait_send()
 
 
 def local(
@@ -414,26 +465,31 @@
             pltpu.VMEM((2, GROUP * C, width), BF16),
             pltpu.VMEM((2, T, feat), BF16),
             pltpu.VMEM((2, 3 * T, 2 * feat), BF16),
-            pltpu.VMEM((GROUP * C, feat), BF16),
-            pltpu.VMEM((groups, GROUP * C, feat), BF16),
-            pltpu.VMEM((groups, n_head, GROUP * C, feat), BF16),
-            pltpu.VMEM((groups, n_head, GROUP * C, feat), BF16),
-            pltpu.VMEM((cols, n_head, C, feat), BF16),
-            pltpu.VMEM((cols, n_head, C, feat), BF16),
-            pltpu.VMEM((cols, C, feat // 2), F32),
-            pltpu.VMEM((cols, C // 2, feat), BF16),
-            pltpu.VMEM((cols, C // 2, feat), BF16),
+            pltpu.VMEM((2, T, feat), BF16),
+            pltpu.VMEM((2, groups, C, feat), BF16),
+            pltpu.VMEM((groups, frames, rows, feat), BF16),
+            pltpu.VMEM((groups, C, feat), BF16),
+            pltpu.VMEM((groups, n_head, C, feat), BF16),
+            pltpu.VMEM((groups, n_head, C, feat), BF16),
+            pltpu.VMEM((groups, n_head, C, feat), BF16),
+            pltpu.VMEM((groups, n_head, C, feat), BF16),
+            pltpu.VMEM((groups, C // 2, feat), BF16),
+            pltpu.VMEM((groups, C // 2, feat), BF16),
             dma((20,)),
             dma((n_head, cols)),
             dma((n_head, cols)),
             dma((2, groups, 2)),
             dma((2, groups, 2)),
+            dma((2, groups)),
+            dma((2, groups)),
+            dma((groups,)),
+            dma((groups,)),
             dma((groups, n_head)),
             dma((groups, n_head)),
-            dma((cols, n_head)),
-            dma((cols, n_head)),
-            dma((cols,)),
-            dma((cols,)),
+            dma((groups, n_head)),
+            dma((groups, n_head)),
+            dma((groups,)),
+            dma((groups,)),
         ],
         compiler_params=pltpu.CompilerParams(
             collective_id=0, has_side_effects=True, vmem_limit_bytes=58 * 1024 * 1024

time: 83.8 us -> 75.5 us (0.901)
  the two profiles are of different devices: /device:TPU:102 before, /device:TPU:1 now
where the time goes in v5:
time: 75.5 us; the launch traced here: 75.3 us
  Pallas kernels  71 us (94%)
  local copies, waits for them, and re-layouts  2.3 us (3%)
  between operations  1.96 us (3%)
    pallas_call x1, Pallas kernels, local(): pl.pallas_call(functools.partial(kernel, (frames, rows, cols, feat, n_lon...  71 us
    unnamed x1, local copies, waits for them, and re-layouts  1.69 us

profile of v5, /device:TPU:1, one launch (start us, length us, event | category | flops | bytes accessed | tf_op | source)
XLA Modules:
  0.0 75.3 jit_solution(5665235557300636225)
XLA Ops:
  2.0 0.6 broadcast_in_dim.2.freq_ref
  2.6 71.0 %shard_map.154 = bf16[2,6,48,192]{3,2,1,0:T(8,128)(2,1)} custom-call(bf16[2,6,48,384]{3,2,1,0:T(8,128)(2,1)} %bitcast.6, s32[1]{0:T(128)S(6)} %copy.18.step_ref, s32[1]{0:T(128)S(6)} %copy.19.num_ref, s32[1]{0:T(128)S(6)} %copy.20.den_ref, s32[6,2,48]{2,1,0:T(2,128)} %bitcast.7, f32[16,128]{1,0:T(8,128)} %broadcast_in_dim.2.freq_ref, ...), custom_call_target="tpu_custom_call" | custom-call | tf_op jit(solution)/shard_map/pallas_call | solution.py:454
  73.6 1.7 %copy.21 = bf16[2,48,6,192]{3,1,2,0:T(8,128)(2,1)} copy(bf16[2,48,6,192]{3,1,2,0:T(8,128)(2,1)} %bitcast.5) | data formatting | bytes 442368
  (1 shorter events, 0.0 us)

commit v6 on v5

--- a/solution.py
+++ b/solution.py
@@ -3,6 +3,7 @@
 
 import jax
 import jax.numpy as jnp
+import numpy as np
 from jax import lax
 from jax.experimental import pallas as pl
 from jax.experimental.pallas import tpu as pltpu
@@ -231,11 +232,15 @@
         query = jnp.dot(normed, wqkv[branch, :, :feat], preferred_element_type=F32)
         q[branch, pl.ds(pl.multiple_of(g * G, G), G), :] = (query * (math.log2(math.e) / math.sqrt(HD))).astype(BF16)
 
-    def my_col(j):
-        return j * GROUP + cfg
-
-    def other_col(j):
-        return j * GROUP + 1 - cfg
+    order_cols = [jnp.where(core == 0, cols - 1 - p, p) for p in range(cols)]
+    cond_cols = [order_cols[p] for p in (2, 4, 5)]
+    uncond_cols = [order_cols[p] for p in (0, 1, 3)]
+
+    def my_col(n):
+        return jnp.where(is_cond, cond_cols[n], uncond_cols[n])
+
+    def other_col(n):
+        return jnp.where(is_cond, uncond_cols[n], cond_cols[n])
 
     def col_rows(c):
         return pl.ds(pl.multiple_of(c * C, C), C)
@@ -252,7 +257,7 @@
     for j in range(groups):
         share_x(j).start()
 
-    angles = freq_ref[...] * step_ref[0].astype(F32)
+    angles = jnp.broadcast_to(freq_ref[...], (16, FREQ // 2)) * step_ref[0].astype(F32)
     temb = jnp.concatenate([jnp.cos(angles), jnp.sin(angles)], axis=1).astype(BF16)
     loads[0].wait()
     mod[...] = jnp.dot(temb, tw[...], preferred_element_type=F32)
@@ -337,65 +342,79 @@
         out_ref[:, other_col(j)] = other.reshape(frames, rows, half_feat)
 
     near = 2 * cols + 1
-    n_keys = (near + GROUP - 1) * C
-
-    def attend(branch, j):
-        r0 = pl.multiple_of(j * G, G)
+
+    def attend(branch, c, count):
+        here = pl.ds(pl.multiple_of(c * C, C), count * C)
+        keys = pl.ds(pl.multiple_of(c * C, C), (near + count - 1) * C)
         for p in range(feat // PAIR):
             sl = pl.ds(p * PAIR, PAIR)
-            att[branch, pl.ds(r0, G), sl] = attend_pair(
-                q[branch, pl.ds(r0, G), sl],
-                kv[branch, pl.ds(r0, n_keys), sl],
-                kv[branch, pl.ds(r0, n_keys), pl.ds(feat + p * PAIR, PAIR)],
-                GROUP,
+            att[branch, here, sl] = attend_pair(
+                q[branch, here, sl],
+                kv[branch, keys, sl],
+                kv[branch, keys, pl.ds(feat + p * PAIR, PAIR)],
+                count,
                 near,
             )
-        share(branch, j).start()
 
     first = jnp.where(is_cond, CTRL, BASE)
     for g in range(groups):
         wait_halo(first, g, 1 - core)
 
-    for j in order:
+    for i, j in enumerate(order):
         wait_halo(first, j, core)
-        attend(first, j)
+        attend(first, j * GROUP, GROUP)
 
         @pl.when(is_cond)
         def _():
-            ctrl_out(j, att[CTRL, col_rows(my_col(j)), :])
+            for n in ((0, 1), (2,), ())[i]:
+                share(CTRL, n).start()
+            for n in ((), (0,), (1, 2))[i]:
+                ctrl_out(n, att[CTRL, col_rows(my_col(n)), :])
+
+        @pl.when(jnp.logical_not(is_cond))
+        def _():
+            for n in ((), (0,), (1, 2))[i]:
+                share(BASE, n).start()
+
+    for n in range(groups):
+        share_x(n).wait_recv()
+
+    def complete(n):
+        collect(n)
+        share(BASE, n).wait_recv()
+        final_out(n)
 
     @pl.when(jnp.logical_not(is_cond))
     def _():
-        for j in order:
-            share(CTRL, j).wait_recv()
-            ctrl_out(j, att_in[CTRL, j])
+        for n in range(groups):
+            share(CTRL, n).wait_recv()
+            ctrl_out(n, att_in[CTRL, n])
+        for n in range(groups):
+            complete(n)
 
     @pl.when(is_cond)
     def _():
         for g in range(groups):
             wait_halo(BASE, g, 1 - core)
-
-    for j in range(groups):
-        share_x(j).wait_recv()
-
-    for i, j in enumerate(order):
-
-        @pl.when(is_cond)
-        def _():
-            wait_halo(BASE, j, core)
-            attend(BASE, j)
-
-        collect(j)
-        share(BASE, j).wait_recv()
-        final_out(j)
-        if i >= 2:
-            reduce(order[i - 2])
-
-    for j in order[groups - 2 :]:
-        reduce(j)
-
-    for j in order:
-        finish(j)
+        wait_halo(BASE, order[0], core)
+        attend(BASE, order[0] * GROUP, GROUP)
+        share(BASE, 0).start()
+        share(BASE, 1).start()
+        wait_halo(BASE, order[1], core)
+        attend(BASE, order[1] * GROUP, GROUP)
+        share(BASE, 2).start()
+        complete(0)
+        wait_halo(BASE, order[2], core)
+        attend(BASE, order_cols[4], 1)
+        complete(1)
+        attend(BASE, order_cols[5], 1)
+        complete(2)
+
+    for n in range(groups):
+        reduce(n)
+
+    for n in range(groups):
+        finish(n)
 
     for c in range(cols):
         gather(c, 1).wait_send()
@@ -444,8 +463,8 @@
     frames, cols, rows, feat = x.shape
     n_lon, n_head = lax.axis_size("lon"), lax.axis_size("head")
     C, T, width = frames * rows, frames * rows * cols, feat * n_head
-    freqs = jnp.exp(-math.log(10000.0) * jnp.arange(FREQ // 2).astype(F32) / (FREQ // 2))
-    freqs = jnp.broadcast_to(freqs[None, :], (16, FREQ // 2))
+    freqs = np.exp(-math.log(10000.0) * np.arange(FREQ // 2) / (FREQ // 2)).astype(np.float32)
+    freqs = jnp.asarray(freqs[None, :])
     dma = pltpu.SemaphoreType.DMA
     vmem = pl.BlockSpec(memory_space=pltpu.VMEM)
     smem = pl.BlockSpec(memory_space=pltpu.SMEM)

time: 75.5 us -> 75 us (level)
  no operation moved by 1% of the time
where the time goes in v6:
time: 75 us; the launch traced here: 74.8 us
  Pallas kernels  71.2 us (95%)
  between operations  1.95 us (3%)
  local copies, waits for them, and re-layouts  1.69 us (2%)
    pallas_call x1, Pallas kernels, local(): pl.pallas_call(functools.partial(kernel, (frames, rows, cols, feat, n_lon...  71.2 us
    unnamed x1, local copies, waits for them, and re-layouts  1.69 us

profile of v6, /device:TPU:1, one launch (start us, length us, event | category | flops | bytes accessed | tf_op | source)
XLA Modules:
  0.0 74.8 jit_solution(15354631591111255103)
XLA Ops:
  1.9 71.2 %shard_map.163 = bf16[2,6,48,192]{3,2,1,0:T(8,128)(2,1)} custom-call(bf16[2,6,48,384]{3,2,1,0:T(8,128)(2,1)} %bitcast.6, s32[1]{0:T(128)S(6)} %copy.19.step_ref, s32[1]{0:T(128)S(6)} %copy.20.num_ref, s32[1]{0:T(128)S(6)} %copy.21.den_ref, s32[6,2,48]{2,1,0:T(2,128)} %bitcast.7, f32[1,128]{1,0:T(1,128)} %constant.2.clone.freq_ref, ...), custom_call_target="tpu_custom_call" | custom-call | tf_op jit(solution)/shard_map/pallas_call | solution.py:473
  73.1 1.7 %copy.22 = bf16[2,48,6,192]{3,1,2,0:T(8,128)(2,1)} copy(bf16[2,48,6,192]{3,1,2,0:T(8,128)(2,1)} %bitcast.5) | data formatting | bytes 442368

commit v7 on v6

--- a/solution.py
+++ b/solution.py
@@ -180,8 +180,8 @@
         gathered(make_cols[i], 1, 3).wait_recv()
         gathered(make_cols[i], 3, 1).wait_recv()
         relay(make_cols[i], 1 if i % 2 == 0 else 3).start()
-        if i + 3 < cols:
-            own_sends(i + 3)
+        if i + 4 < cols:
+            own_sends(i + 4)
 
     def own_rows(g):
         return pl.ds(pl.multiple_of(T + g * G, G), G)
@@ -192,6 +192,10 @@
         return send(
             kv.at[branch, own_rows(g)], kv.at[branch, dst], h_send.at[branch, g, side], h_recv.at[branch, g, side], who
         )
+
+    def send_halo(branch, g):
+        for side in range(2):
+            halo(branch, g, side).start()
 
     def wait_halo(branch, g, side):
         dst = pl.ds(pl.multiple_of(2 * T * side + g * G, G), G)
@@ -227,8 +231,14 @@
         kv[branch, own_rows(g), :] = jnp.dot(
             normed, wqkv[branch, :, feat:], preferred_element_type=F32
         ).astype(BF16)
-        for side in range(2):
-            halo(branch, g, side).start()
+        if branch == CTRL:
+            send_halo(branch, g)
+        else:
+
+            @pl.when(jnp.logical_not(is_cond))
+            def _():
+                send_halo(branch, g)
+
         query = jnp.dot(normed, wqkv[branch, :, :feat], preferred_element_type=F32)
         q[branch, pl.ds(pl.multiple_of(g * G, G), G), :] = (query * (math.log2(math.e) / math.sqrt(HD))).astype(BF16)
 
@@ -252,7 +262,7 @@
         src = att.at[branch, col_rows(other_col(j))]
         return send(src, att_in.at[branch, j], a_send.at[branch, j], a_recv.at[branch, j], to_cfg)
 
-    for i in range(3):
+    for i in range(4):
         own_sends(i)
     for j in range(groups):
         share_x(j).start()
@@ -265,14 +275,15 @@
     ratio = (ones * num_ref[0].astype(F32)) / (ones * den_ref[0].astype(F32))
     ratio = ratio[0:1, :]
     factor = jnp.where(is_cond, ratio, 1.0 - ratio)
-    own_copy.wait()
-    for copy in loads[1:]:
-        copy.wait()
 
     for i, g in enumerate(make):
         until = min(cols, (i + 2) * GROUP)
         for n in range(0 if i == 0 else min(cols, (i + 1) * GROUP), until):
             serve(n)
+        if i == 0:
+            own_copy.wait()
+            for copy in loads[1:]:
+                copy.wait()
         for c in make_cols[i * GROUP : (i + 1) * GROUP]:
             gathered(c, 2, 2).wait_recv()
 
@@ -281,6 +292,11 @@
             project(CTRL, g)
 
         project(BASE, g)
+
+    @pl.when(is_cond)
+    def _():
+        for g in make:
+            send_halo(BASE, g)
 
     def ctrl_sum(j, k):
         return to_peer(part.at[j, k], parts_in.at[j, n_head - k], p_send.at[j, k], p_recv.at[j, n_head - k], k)
@@ -333,13 +349,13 @@
         other = jnp.where(is_cond, high, low).astype(BF16)
         swap_out[j] = jnp.concatenate([other[: C // 2], other[C // 2 :]], axis=1)
         swap(j).start()
-        out_ref[:, c] = jnp.where(is_cond, low, high).astype(BF16).reshape(frames, rows, half_feat)
+        out_ref[:, c] = jnp.where(is_cond, low, high).reshape(frames, rows, half_feat)
 
     def finish(j):
         swap(j).wait_recv()
         other = swap_in[j]
         other = jnp.concatenate([other[:, :half_feat], other[:, half_feat:]], axis=0)
-        out_ref[:, other_col(j)] = other.reshape(frames, rows, half_feat)
+        out_ref[:, other_col(j)] = other.astype(F32).reshape(frames, rows, half_feat)
 
     near = 2 * cols + 1
 
@@ -472,7 +488,7 @@
     groups = cols // GROUP
     out = pl.pallas_call(
         functools.partial(kernel, (frames, rows, cols, feat, n_lon, n_head)),
-        out_shape=jax.ShapeDtypeStruct((frames, cols, rows, feat // 2), BF16),
+        out_shape=jax.ShapeDtypeStruct((frames, cols, rows, feat // 2), F32),
         in_specs=[hbm, smem, smem, smem, vmem, vmem, vmem] + [hbm] * 10,
         out_specs=vmem,
         scratch_shapes=[
@@ -532,7 +548,7 @@
         ctrl_o,
         zero_linear,
     )
-    return out.transpose(0, 2, 1, 3)
+    return out.transpose(0, 2, 1, 3).astype(BF16)
 
 
 def solution(mesh):

time: 75 us -> 77.8 us (1.037)
  the two profiles are of different devices: /device:TPU:1 before, /device:TPU:2 now
where the time goes in v7:
time: 77.8 us; the launch traced here: 77.6 us
  Pallas kernels  73.9 us (95%)
  between operations  1.95 us (3%)
  other arithmetic  1.81 us (2%)
    pallas_call x1, Pallas kernels, local(): pl.pallas_call(functools.partial(kernel, (frames, rows, cols, feat, n_lon...  73.9 us
    convert_element_type x1, other arithmetic, local(): return out.transpose(0, 2, 1, 3).astype(BF16)  1.81 us

profile of v7, /device:TPU:2, one launch (start us, length us, event | category | flops | bytes accessed | tf_op | source)
XLA Modules:
  0.0 77.6 jit_solution(6834962481884333015)
XLA Ops:
  1.9 73.9 %shard_map.163 = f32[2,6,48,192]{3,2,1,0:T(8,128)} custom-call(bf16[2,6,48,384]{3,2,1,0:T(8,128)(2,1)} %bitcast.6, s32[1]{0:T(128)S(6)} %copy.18.step_ref, s32[1]{0:T(128)S(6)} %copy.19.num_ref, s32[1]{0:T(128)S(6)} %copy.20.den_ref, s32[6,2,48]{2,1,0:T(2,128)} %bitcast.7, f32[1,128]{1,0:T(1,128)} %constant.2.clone.freq_ref, bf16[16,1536]{1,0:T(8,128)(2,1)} %table_ref.1, ...), custom_call_target="tpu_custom_call" | custom-call | tf_op jit(solution)/shard_map/pallas_call | solution.py:489
  75.8 1.8 %convert_bitcast_fusion = bf16[2,48,6,192]{3,1,2,0:T(8,128)(2,1)} fusion(f32[2,6,48,192]{3,2,1,0:T(8,128)} %shard_map.163), kind=kLoop, calls=%fused_computation | loop fusion | flops 110592 | bytes 663552 | tf_op jit(solution)/shard_map/convert_element_type | solution.py:551

commit v8 on v7

--- a/solution.py
+++ b/solution.py
@@ -290,13 +290,14 @@
         @pl.when(is_cond)
         def _():
             project(CTRL, g)
+            if i >= 1:
+                send_halo(BASE, make[i - 1])
 
         project(BASE, g)
 
     @pl.when(is_cond)
     def _():
-        for g in make:
-            send_halo(BASE, g)
+        send_halo(BASE, make[groups - 1])
 
     def ctrl_sum(j, k):
         return to_peer(part.at[j, k], parts_in.at[j, n_head - k], p_send.at[j, k], p_recv.at[j, n_head - k], k)
@@ -349,13 +350,13 @@
         other = jnp.where(is_cond, high, low).astype(BF16)
         swap_out[j] = jnp.concatenate([other[: C // 2], other[C // 2 :]], axis=1)
         swap(j).start()
-        out_ref[:, c] = jnp.where(is_cond, low, high).reshape(frames, rows, half_feat)
+        out_ref[:, c] = jnp.where(is_cond, low, high).astype(BF16).reshape(frames, rows, half_feat)
 
     def finish(j):
         swap(j).wait_recv()
         other = swap_in[j]
         other = jnp.concatenate([other[:, :half_feat], other[:, half_feat:]], axis=0)
-        out_ref[:, other_col(j)] = other.astype(F32).reshape(frames, rows, half_feat)
+        out_ref[:, other_col(j)] = other.reshape(frames, rows, half_feat)
 
     near = 2 * cols + 1
 
@@ -488,7 +489,7 @@
     groups = cols // GROUP
     out = pl.pallas_call(
         functools.partial(kernel, (frames, rows, cols, feat, n_lon, n_head)),
-        out_shape=jax.ShapeDtypeStruct((frames, cols, rows, feat // 2), F32),
+        out_shape=jax.ShapeDtypeStruct((frames, cols, rows, feat // 2), BF16),
         in_specs=[hbm, smem, smem, smem, vmem, vmem, vmem] + [hbm] * 10,
         out_specs=vmem,
         scratch_shapes=[
@@ -548,7 +549,7 @@
         ctrl_o,
         zero_linear,
     )
-    return out.transpose(0, 2, 1, 3).astype(BF16)
+    return out.transpose(0, 2, 1, 3)
 
 
 def solution(mesh):

time: 77.8 us -> 77.1 us (level)
  other arithmetic: 1.81 us -> 0 us
  local copies, waits for them, and re-layouts: 0 us -> 1.69 us
    convert_element_type x1 -> x0, other arithmetic: 1.81 us -> none  [local(): return out.transpose(0, 2, 1, 3).astype(BF16)]
    unnamed x0 -> x1, local copies, waits for them, and re-layouts: none -> 1.69 us
where the time goes in v8:
time: 77.1 us; the launch traced here: 76.9 us
  Pallas kernels  73.2 us (95%)
  between operations  1.95 us (3%)
  local copies, waits for them, and re-layouts  1.69 us (2%)
    pallas_call x1, Pallas kernels, local(): pl.pallas_call(functools.partial(kernel, (frames, rows, cols, feat, n_lon...  73.2 us
    unnamed x1, local copies, waits for them, and re-layouts  1.69 us

profile of v8, /device:TPU:2, one launch (start us, length us, event | category | flops | bytes accessed | tf_op | source)
XLA Modules:
  0.0 76.9 jit_solution(16337300179189091699)
XLA Ops:
  1.9 73.2 %shard_map.163 = bf16[2,6,48,192]{3,2,1,0:T(8,128)(2,1)} custom-call(bf16[2,6,48,384]{3,2,1,0:T(8,128)(2,1)} %bitcast.6, s32[1]{0:T(128)S(6)} %copy.19.step_ref, s32[1]{0:T(128)S(6)} %copy.20.num_ref, s32[1]{0:T(128)S(6)} %copy.21.den_ref, s32[6,2,48]{2,1,0:T(2,128)} %bitcast.7, f32[1,128]{1,0:T(1,128)} %constant.2.clone.freq_ref, ...), custom_call_target="tpu_custom_call" | custom-call | tf_op jit(solution)/shard_map/pallas_call | solution.py:490
  75.2 1.7 %copy.22 = bf16[2,48,6,192]{3,1,2,0:T(8,128)(2,1)} copy(bf16[2,48,6,192]{3,1,2,0:T(8,128)(2,1)} %bitcast.5) | data formatting | bytes 442368
